TPU v7x, 128 devices: a whole 4x4x4 slice. The times are simulated.
128 devices in a mesh: dp: 4 (over x), pipe: 2 (over z_hi), tensor: 16 (over z_lo, y, core).
Axes of the slice: x: 4, y: 4, z: 4 (z_hi: 2, z_lo: 2; z = z_hi * 2 + z_lo), core: 2. Of those that a mesh axis runs over, the one named last changes fastest.
Arguments:
- activations: bfloat16 [4, 256, 12288], P(None, 'dp', 'tensor'), may hold values from -40 to 40
- gains: float32 [2, 12288], P('pipe', 'tensor'), may hold values from 0.1 to 1.9
- block_values: bfloat16 [2, 192, 48, 4096], P('pipe', 'tensor'), may hold values from -0.109375 to 0.109375
- block_rows: int32 [2, 192, 48], P('pipe', 'tensor'), may hold values from 0 to 191, as said below
Outputs:
- hessians: float32 [2, 12288, 12288], P('pipe', 'dp', 'tensor')
- sections: bfloat16 [2, 4, 256, 12288], P('pipe', None, 'dp', 'tensor')
Inputs may be any that keep to these rules, and one draw needn't show every extreme that they name: `block_rows`: for each section and column block the 48 row-block numbers are distinct.
All inputs are finite; a program needn't handle non-finite values.
Results may differ from a plain program's by a relative error of at most 0.009.
Values may be sent and summed in bfloat16 or wider, within the bound.
No kernel may reach another device: no remote copies, remote signals or barrier semaphores. Data moves between devices by JAX's collectives and lax.ppermute only.
A program may use at most 192 MiB of HBM per device.

v0:
```python
import jax
import jax.numpy as jnp
from jax import lax
from jax.experimental import pallas as pl
from jax.experimental.pallas import tpu as pltpu
from jax.sharding import PartitionSpec as P

D = 12288
BLOCK = 64
KEEP = 48
M = 4
TOK = 64
ROWS = M * TOK
DP = 4
TENSOR = 16
WIDTH = D // TENSOR
QUARTER = D // DP
EPSILON = 1e-05
LANES = 128
SPAN = 256
CHUNK = 64
MIB = 1024 * 1024
VMEM_LIMIT = 61 * MIB
NEAR = [(dz, dy) for dz in range(2) for dy in range(4)]
ANY = pl.BlockSpec(memory_space=pl.ANY)
VMEM = pl.BlockSpec(memory_space=pltpu.VMEM)
SMEM = pl.BlockSpec(memory_space=pltpu.SMEM)


def build_kernel(rows_ref, blocks_ref, dense_ref):
    group = pl.program_id(0)

    @pl.loop(0, D // SPAN)
    def _(chunk):
        dense_ref[0, pl.ds(pl.multiple_of(chunk * SPAN, SPAN), SPAN), :] = jnp.zeros((SPAN, SPAN), jnp.bfloat16)

    per = SPAN // BLOCK

    @pl.loop(0, KEEP, unroll=4)
    def _(kept):
        for part in range(per):
            first = pl.multiple_of(rows_ref[per * group + part, kept] * BLOCK, BLOCK)
            dense_ref[0, pl.ds(first, BLOCK), part * BLOCK:(part + 1) * BLOCK] = blocks_ref[part, kept]


def build_dense(values, rows_index):
    blocks = values.reshape(WIDTH // BLOCK, KEEP, BLOCK, BLOCK)
    per = SPAN // BLOCK
    return pl.pallas_call(
        build_kernel,
        grid_spec=pltpu.PrefetchScalarGridSpec(
            num_scalar_prefetch=1,
            grid=(WIDTH // SPAN,),
            in_specs=[pl.BlockSpec((per, KEEP, BLOCK, BLOCK), lambda group, rows: (group, 0, 0, 0))],
            out_specs=pl.BlockSpec((1, D, SPAN), lambda group, rows: (group, 0, 0)),
        ),
        out_shape=jax.ShapeDtypeStruct((WIDTH // SPAN, D, SPAN), jnp.bfloat16),
        compiler_params=pltpu.CompilerParams(vmem_limit_bytes=VMEM_LIMIT),
        cost_estimate=pl.CostEstimate(flops=0, bytes_accessed=32 * MIB, transcendentals=0),
        name="build_dense",
    )(rows_index, blocks)


def start_pieces(pieces, refs, rows, sems):
    for array, start, count, position, into in pieces:
        pltpu.make_async_copy(
            refs[array].at[pl.ds(start, count)], rows.at[position, pl.ds(into, count)], sems.at[position]
        ).start()


def wait_block(rows, sems, position):
    pltpu.make_async_copy(rows.at[position], rows.at[position], sems.at[position]).wait()


def spread(column, means, span):
    means[span] = jnp.broadcast_to(column, (ROWS, LANES))


def block_at(spot_ref, position):
    z = lax.rem(spot_ref[1] + lax.rem(position // 4, 2), 2)
    y = lax.rem(spot_ref[2] + lax.rem(position, 4), 4)
    core = lax.rem(spot_ref[3] + position // len(NEAR), 2)
    return z * 8 + y * 2 + core


def layer_kernel(pieces, count, straight, spot_ref, weight_ref, gains_ref, own_ref, *refs):
    sources, (out_ref, stats_ref, rows, weight, total, means, scales, sems, weight_sems) = refs[:count], refs[count:]

    def place(position):
        return position if straight else block_at(spot_ref, position)

    def weight_copy(position):
        span = pl.ds(pl.multiple_of(place(position) * WIDTH, WIDTH), WIDTH)
        into = pl.ds(pl.multiple_of(position * WIDTH, WIDTH), WIDTH)
        return pltpu.make_async_copy(weight_ref.at[:, span], weight.at[:, into], weight_sems.at[position])

    start_pieces(pieces, sources, rows, sems)
    means[...] = jnp.zeros_like(means)
    scales[...] = jnp.zeros_like(scales)
    total[...] = own_ref[...].astype(jnp.float32)
    @pl.loop(0, TENSOR // 2)
    def _(pair):
        for position in (2 * pair, 2 * pair + 1):
            wait_block(rows, sems, position)
            for chunk in range(0, ROWS, CHUNK):
                span = slice(chunk, chunk + CHUNK)
                added = jnp.zeros((CHUNK, LANES), jnp.float32)
                squared = added
                for part in range(WIDTH // LANES):
                    values = rows[position, span, part * LANES:(part + 1) * LANES].astype(jnp.float32)
                    added = added + values
                    squared = squared + values * values
                means[span] += added
                scales[span] += squared
        weight_copy(pair).start()

    mean = jnp.sum(means[...], axis=1, keepdims=True) / D
    square = jnp.sum(scales[...], axis=1, keepdims=True) / D
    scale = lax.rsqrt(square - mean * mean + EPSILON)
    lane = lax.broadcasted_iota(jnp.int32, (ROWS, LANES), 1)
    stats_ref[...] = jnp.transpose(jnp.where(lane == 0, mean, scale))[:8]
    spread(mean, means, slice(0, ROWS))
    spread(scale, scales, slice(0, ROWS))

    def normalise(position):
        gain = gains_ref[place(position)]
        for chunk in range(0, ROWS, CHUNK):
            span = slice(chunk, chunk + CHUNK)
            for part in range(WIDTH // LANES):
                lanes = slice(part * LANES, (part + 1) * LANES)
                values = rows[position, span, lanes].astype(jnp.float32)
                scaled = (values - means[span]) * scales[span] * gain[:, lanes]
                rows[position, span, lanes] = scaled.astype(jnp.bfloat16)

    normalise(0)
    normalise(1)

    @pl.loop(0, TENSOR // 2)
    def _(pair):
        position = 2 * pair
        for later in range(2):

            @pl.when(position + TENSOR // 2 + later < TENSOR)
            def _():
                weight_copy(position + TENSOR // 2 + later).start()

        weight_copy(position).wait()
        weight_copy(position + 1).wait()
        left = jnp.concatenate([rows[position], rows[position + 1]], axis=1)
        span = pl.ds(pl.multiple_of(position * WIDTH, 2 * WIDTH), 2 * WIDTH)
        for group in range(WIDTH // SPAN):
            lanes = slice(group * SPAN, (group + 1) * SPAN)
            total[:, lanes] += jnp.dot(left, weight[group, span], preferred_element_type=jnp.float32)

        @pl.when(position + 2 < TENSOR)
        def _():
            normalise(position + 2)
            normalise(position + 3)

    out_ref[...] = total[...].astype(jnp.bfloat16)


def in_hbm(arrays):
    return [pltpu.with_memory_space_constraint(array, pltpu.HBM) for array in arrays]


def layer(spot, gathered, pieces, weight, gains, own, straight):
    count = len(gathered)
    return pl.pallas_call(
        lambda *refs: layer_kernel(pieces, count, straight, *refs),
        in_specs=[SMEM, ANY, VMEM, VMEM] + [ANY] * count,
        out_specs=[VMEM, VMEM],
        out_shape=[
            jax.ShapeDtypeStruct((ROWS, WIDTH), jnp.bfloat16),
            jax.ShapeDtypeStruct((8, ROWS), jnp.float32),
        ],
        scratch_shapes=[
            pltpu.VMEM((TENSOR, ROWS, WIDTH), jnp.bfloat16),
            pltpu.VMEM((WIDTH // SPAN, D, SPAN), jnp.bfloat16),
            pltpu.VMEM((ROWS, WIDTH), jnp.float32),
            pltpu.VMEM((ROWS, LANES), jnp.float32),
            pltpu.VMEM((ROWS, LANES), jnp.float32),
            pltpu.SemaphoreType.DMA((TENSOR,)),
            pltpu.SemaphoreType.DMA((TENSOR,)),
        ],
        compiler_params=pltpu.CompilerParams(vmem_limit_bytes=VMEM_LIMIT),
        cost_estimate=pl.CostEstimate(flops=2 * ROWS * D * WIDTH, bytes_accessed=2 * D * (WIDTH + ROWS), transcendentals=ROWS),
        name="layer",
    )(spot, *in_hbm([weight]), gains, own, *in_hbm(gathered))


PIECE = 384
PER = WIDTH // PIECE
HALF = TENSOR // DP // 2
CLASSES = [(side, half) for side in range(2) for half in range(HALF)]


def half_at(spot_ref, step):
    return spot_ref[1] if step == 2 else lax.rem(spot_ref[2], 2)


def pick_kernel(pieces, count, spot_ref, *refs):
    sources, picked, sems = refs[:count], refs[count + 1:-1], refs[-1]
    jobs = [(0, 0, 0), (0, 1, 1)] + [(step, half_at(spot_ref, step), 0) for step in range(1, DP)]
    for job, (step, half, into) in enumerate(jobs):
        target = lax.rem(spot_ref[0] + step, DP)
        dz = lax.rem(target // 2 + 2 - spot_ref[1], 2)
        dy = lax.rem(lax.rem(target, 2) * 2 + half + 4 - spot_ref[2], 4)
        for position in range(len(NEAR)):

            @pl.when(dz * 4 + dy == position)
            def _():
                for array, start, size, at, row in pieces:
                    if at == position:
                        pltpu.make_async_copy(
                            sources[array].at[pl.ds(start, size)],
                            picked[step].at[pl.ds(into * ROWS + row, size)],
                            sems.at[job],
                        ).start()

    for job, (step, _, into) in enumerate(jobs):
        block = picked[step].at[pl.ds(into * ROWS, ROWS)]
        pltpu.make_async_copy(block, block, sems.at[job]).wait()


def pick(spot, gathered, pieces, before):
    count = len(gathered)
    return pl.pallas_call(
        lambda *refs: pick_kernel(pieces, count, *refs),
        in_specs=[SMEM] + [ANY] * (count + 1),
        out_specs=[VMEM] * DP,
        out_shape=[jax.ShapeDtypeStruct((rows, WIDTH), jnp.bfloat16) for rows in [HALF * ROWS] + [ROWS] * (DP - 1)],
        scratch_shapes=[pltpu.SemaphoreType.DMA((DP + 1,))],
        compiler_params=pltpu.CompilerParams(vmem_limit_bytes=VMEM_LIMIT),
        cost_estimate=pl.CostEstimate(flops=0, bytes_accessed=4 * (DP + 1) * ROWS * WIDTH, transcendentals=0),
        name="pick",
    )(spot, *in_hbm(gathered), before)


def after(values, others):
    count = len(values)
    return pl.pallas_call(
        lambda *refs: None,
        in_specs=[ANY] * (count + len(others)),
        out_specs=[ANY] * count,
        out_shape=[jax.ShapeDtypeStruct(value.shape, value.dtype) for value in values],
        input_output_aliases={place: place for place in range(count)},
        name="after",
    )(*in_hbm(values), *others)


def gram_kernel(spot_ref, *refs):
    near, far, refs = refs[:2 * DP], refs[2 * DP:4 * DP - 2], refs[4 * DP - 2:]
    stats_refs, refs = refs[:DP], refs[DP:]
    cols_ref, gains_ref, col_gain_ref, out_ref, rows, cols, means, scales, left, result, sems, row_sems = refs

    def block_of(group):
        return lax.rem(spot_ref[3] + group // HALF, 2) + 2 * lax.rem(group, HALF)

    def row_copy(source, group, part):
        return pltpu.make_async_copy(source, rows.at[group, part], row_sems.at[group, part])

    def start_rows(side):
        for half in range(HALF):
            row_copy(near[side * DP].at[pl.ds(half * ROWS, ROWS)], side * HALF + half, 0).start()
        for part in range(1, DP):
            half = half_at(spot_ref, part)
            row_copy(near[side * DP + part], side * HALF + half, part).start()
            row_copy(far[side * (DP - 1) + part - 1], side * HALF + 1 - half, part).start()

    start_rows(0)
    for part in range(DP):
        span = slice(part * ROWS, (part + 1) * ROWS)
        means[span] = jnp.transpose(jnp.broadcast_to(stats_refs[part][0:1], (LANES, ROWS)))
        scales[span] = jnp.transpose(jnp.broadcast_to(stats_refs[part][1:2], (LANES, ROWS)))
        for chunk in range(0, ROWS, CHUNK):
            span = slice(part * ROWS + chunk, part * ROWS + chunk + CHUNK)
            for lane in range(WIDTH // LANES):
                lanes = slice(lane * LANES, (lane + 1) * LANES)
                values = cols_ref[lax.rem(spot_ref[0] + DP - part, DP), chunk:chunk + CHUNK, lanes].astype(jnp.float32)
                scaled = (values - means[span]) * scales[span] * col_gain_ref[:, lanes]
                cols[span, lanes] = scaled.astype(jnp.bfloat16)

    def normalise(group, slot):
        if slot == 0:
            for part in range(DP):
                row_copy(rows.at[group, part], group, part).wait()
        gain = gains_ref[spot_ref[0] * (TENSOR // DP) + block_of(group)]
        for part in range(DP):
            for chunk in range(0, ROWS, CHUNK):
                span = slice(part * ROWS + chunk, part * ROWS + chunk + CHUNK)
                for lane in range(PIECE // LANES):
                    first = slot * PIECE + lane * LANES
                    from_lanes = slice(first, first + LANES)
                    values = rows[group, part, chunk:chunk + CHUNK, from_lanes].astype(jnp.float32)
                    scaled = (values - means[span]) * scales[span] * gain[:, from_lanes]
                    left[slot, span, lane * LANES:(lane + 1) * LANES] = scaled.astype(jnp.bfloat16)

    def store(group, slot):
        row = pl.multiple_of(block_of(group) * WIDTH + slot * PIECE, PIECE)
        return pltpu.make_async_copy(result.at[slot], out_ref.at[pl.ds(row, PIECE)], sems.at[slot])

    normalise(0, 0)
    start_rows(1)

    @pl.loop(0, len(CLASSES))
    def _(group):
        for slot in range(PER):
            product = lax.dot_general(
                left[slot], cols[...], (((0,), (0,)), ((), ())), preferred_element_type=jnp.float32
            )

            @pl.when(group > 0)
            def _():
                store(group - 1, slot).wait()

            result[slot] = product * (2.0 / (DP * ROWS))
            store(group, slot).start()
            if slot + 1 < PER:
                normalise(group, slot + 1)
            else:

                @pl.when(group + 1 < len(CLASSES))
                def _():
                    normalise(group + 1, 0)

    for slot in range(PER):
        store(len(CLASSES) - 1, slot).wait()


def gram(spot, near, far, cols, stats, gains, col_gain):
    return pl.pallas_call(
        gram_kernel,
        in_specs=[SMEM] + [ANY] * (4 * DP - 2) + [VMEM] * (DP + 3),
        out_specs=ANY,
        out_shape=jax.ShapeDtypeStruct((QUARTER, WIDTH), jnp.float32),
        scratch_shapes=[
            pltpu.VMEM((len(CLASSES), DP, ROWS, WIDTH), jnp.bfloat16),
            pltpu.VMEM((DP * ROWS, WIDTH), jnp.bfloat16),
            pltpu.VMEM((DP * ROWS, LANES), jnp.float32),
            pltpu.VMEM((DP * ROWS, LANES), jnp.float32),
            pltpu.VMEM((2, DP * ROWS, PIECE), jnp.bfloat16),
            pltpu.VMEM((2, PIECE, WIDTH), jnp.float32),
            pltpu.SemaphoreType.DMA((2,)),
            pltpu.SemaphoreType.DMA((len(CLASSES), DP)),
        ],
        compiler_params=pltpu.CompilerParams(vmem_limit_bytes=VMEM_LIMIT),
        cost_estimate=pl.CostEstimate(
            flops=2 * DP * ROWS * QUARTER * WIDTH, bytes_accessed=4 * QUARTER * WIDTH + 2 * DP * ROWS * (QUARTER + WIDTH), transcendentals=0
        ),
        name="gram",
    )(spot, *near, *far, *stats, cols, gains, col_gain)


def along_dp(value, step):
    return lax.ppermute(value, "dp", [(source, (source + step) % DP) for source in range(DP)])


def gather_dp(value):
    return [value] + [along_dp(value, step) for step in range(1, DP)]


def tensor_at(z, y, core):
    return (z % 2) * 8 + (y % 4) * 2 + core % 2


def shift(value, z, y, core):
    pairs = [
        (tensor_at(a, b, c), tensor_at(a + z, b + y, c + core)) for a in range(2) for b in range(4) for c in range(2)
    ]
    return lax.ppermute(value, "tensor", pairs)


def share(value, step):
    pairs = []
    for z in range(2):
        for y in range(4):
            for core in range(2):
                to = {1: (z, y ^ 1), 2: (1 - z, y), 3: (z, 3 - y)}[step]
                pairs.append((tensor_at(z, y, core), tensor_at(*to, core)))
    return lax.ppermute(value, "tensor", pairs)


def gather_near(value):
    rows = value.shape[0]
    cut, cut2 = rows * 3 // 8, rows * 11 // 16
    up, down, over = shift(value, 0, 1, 0), shift(value, 0, -1, 0), shift(value, 1, 0, 0)
    up2, over_up, over_down = shift(up, 0, 1, 0), shift(up, 1, 0, 0), shift(over, 0, -1, 0)
    far = [
        shift(up2[:cut], 1, 0, 0),
        shift(over_up[cut:cut2], 0, 1, 0),
        shift(over_down[cut2:], 0, -1, 0),
    ]
    mine = [value, down, up2, up, over, over_down, over_up] + far
    theirs = [shift(array, 0, 0, 1) for array in mine]
    pieces = []
    for side in range(2):
        at, pos = side * len(mine), side * len(NEAR)
        pieces += [(at + array, 0, rows, pos + position, 0) for array, position in enumerate([0, 1, 2, 3, 4, 5, 7])]
        pieces += [
            (at + 7, 0, cut, pos + 6, 0),
            (at + 8, 0, cut2 - cut, pos + 6, cut),
            (at + 9, 0, rows - cut2, pos + 6, cut2),
        ]
    return mine + theirs, pieces


def body(activations, gains, block_values, block_rows):
    first = lax.axis_index("pipe") == 0
    quarter = lax.axis_index("dp")
    here = lax.axis_index("tensor")
    gain = gains[0]
    own = activations.reshape(ROWS, WIDTH)
    with jax.named_scope("rows_first"):
        gathered = lax.all_gather(own, "tensor", axis=0, tiled=True)
    with jax.named_scope("gains"):
        all_gains = lax.all_to_all(jnp.broadcast_to(gain[None, :], (TENSOR, WIDTH)), "tensor", 0, 0, tiled=True)
        all_gains = all_gains[:, None, :]
    with jax.named_scope("weight"):
        weight = build_dense(block_values[0], block_rows[0])
    spot = jnp.stack([quarter, here // 8, here // 2 % 4, here % 2]).astype(jnp.int32)
    with jax.named_scope("layer_first"):
        pieces = [(0, block * ROWS, ROWS, block, 0) for block in range(TENSOR)]
        updated_first, _ = layer(spot, [gathered], pieces, weight, all_gains, own, True)
    with jax.named_scope("hand_over"):
        received = lax.ppermute(updated_first, "pipe", [(0, 1)])
    stream = jnp.where(first, own, received)
    with jax.named_scope("columns"):
        cols = lax.all_gather(jnp.where(first, own, 0) + received, "dp", axis=0)
    with jax.named_scope("rows_second"):
        arrays, pieces = gather_near(stream)
    with jax.named_scope("hessian_rows"):
        mine = len(arrays) // 2
        picked = pick(spot, arrays[:mine], [piece for piece in pieces if piece[0] < mine], cols)
        rows = [along_dp(picked[step], step) for step in range(1, DP)]
    with jax.named_scope("layer_second"):
        updated_second, stats = layer(spot, arrays, pieces, weight, all_gains, stream, False)
        stats = gather_dp(stats)
    with jax.named_scope("hessian"):
        near = [picked[0], *after(rows, [stats[0]])]
        far = [share(value, step) for step, value in enumerate(near) if step > 0]
        far[1:2] = after([far[1]], stats[1:])
        near += [shift(value, 0, 0, 1) for value in near]
        far += [shift(value, 0, 0, 1) for value in far]
        hessian = gram(spot, near, far, cols, stats, all_gains, gain[None, :])
    sections = jnp.where(first, updated_first, updated_second)
    return (hessian[None], sections.reshape(1, M, TOK, WIDTH))


def solution(mesh):
    return jax.shard_map(
        body,
        mesh=mesh,
        in_specs=(
            P(None, "dp", "tensor"),
            P("pipe", "tensor"),
            P("pipe", "tensor", None, None),
            P("pipe", "tensor", None),
        ),
        out_specs=(P("pipe", "dp", "tensor"), P("pipe", None, "dp", "tensor")),
        check_vma=False,
    )
```

profile of v0, /device:TPU:1, one launch (start us, length us, event | category | flops | bytes accessed | tf_op | source)
XLA Modules:
  0.0 191.2 jit_solution(17714391925761730558)
XLA Ops:
  7.2 0.7 all-gather.4.cloned.1.call-update
  7.9 0.7 reduce
  8.6 0.6 broadcast_in_dim.13
  9.3 7.3 %all-to-all-start = ((f32[16,1,768]{2,1,0:T(1,128)}), f32[16,1,768]{2,1,0:T(1,128)S(1)}, u32[]{:S(2)}, u32[]{:S(2)}) async-start(f32[16,1,768]{2,1,0:T(1,128)} %broadcast_in_dim.13), calls=%async_computation | async-start | bytes 98304 | tf_op jit(solution)/shard_map/gains/all_to_all | solution.py:417
  16.7 0.7 pad_add_fusion.refs_0_.spot_ref
  17.4 13.8 %squeeze.7.blocks_ref = bf16[12,48,64,64]{3,2,1,0:T(8,128)(2,1)} reshape(bf16[1,12,48,4096]{3,2,1,0:T(8,128)(2,1)} %param.6) | data formatting | bytes 9437184 | tf_op jit(solution)/shard_map/weight/reshape;weight/squeeze | solution.py:47
  31.7 13.8 %build_dense.1.refs_1_ = bf16[3,12288,256]{2,1,0:T(8,128)(2,1)} custom-call(s32[12,48]{1,0:T(8,128)} %bitcast.20, bf16[12,48,64,64]{3,2,1,0:T(8,128)(2,1)} %squeeze.7.blocks_ref), custom_call_target="tpu_custom_call" | custom-call | bytes 33554432 | tf_op jit(solution)/shard_map/weight/build_dense/pallas_call | solution.py:49
  45.5 10.2 %all-gather.4.cloned.1.call-done.refs_4_ = bf16[4096,768]{1,0:T(8,128)(2,1)} async-done(((bf16[256,768]{1,0:T(8,128)(2,1)}), bf16[4096,768]{1,0:T(8,128)(2,1)}) %all-gather.4.cloned.1.call-update) | async-done | bytes 6291472 | tf_op jit(solution)/shard_map/rows_first/all_gather | solution.py:415
  55.8 13.9 %layer.2 = (bf16[256,768]{1,0:T(8,128)(2,1)}, f32[8,256]{1,0:T(8,128)}) custom-call(s32[4]{0:T(128)} %pad_add_fusion.refs_0_.spot_ref, bf16[3,12288,256]{2,1,0:T(8,128)(2,1)} %build_dense.1.refs_1_, f32[16,1,768]{2,1,0:T(1,128)} %copy-done.10, bf16[256,768]{1,0:T(8,128)(2,1)} %bitcast.16, bf16[4096,768]{1,0:T(8,128)(2,1)} %all-gather.4.cloned.1.call-done.refs_4_), custom_call_target="tpu_custom_call" | custom-call | flops 4831838208 | bytes 25165824 | tf_op jit(solution)/shard_map/layer_first/layer/pallas_call | solution.py:169
  69.7 4.6 %collective-permute-start = (bf16[256,768]{1,0:T(8,128)(2,1)}, bf16[256,768]{1,0:T(8,128)(2,1)S(1)}, u32[]{:S(2)}, u32[]{:S(2)}) collective-permute-start(bf16[256,768]{1,0:T(8,128)(2,1)} %get-tuple-element.12), channel_id=1, source_target_pairs={{0,16},{1,17},{2,18},{3,19},{4,20},{5,21},{6,22},{7,23},{8,24},{9,... | collective-permute-start | bytes 1179656 | tf_op jit(solution)/shard_map/hand_over/ppermute | solution.py:426
  74.2 8.5 %collective-permute-done = bf16[256,768]{1,0:T(8,128)(2,1)S(1)} collective-permute-done((bf16[256,768]{1,0:T(8,128)(2,1)}, bf16[256,768]{1,0:T(8,128)(2,1)S(1)}, u32[]{:S(2)}, u32[]{:S(2)}) %collective-permute-start) | collective-permute-done | bytes 393248 | tf_op jit(solution)/shard_map/hand_over/ppermute | solution.py:426
  82.7 0.8 select_add_fusion
  83.6 1.3 collective-permute-start.2
  85.3 1.5 collective-permute-start.1
  86.8 1.9 collective-permute-start.13
  88.7 5.7 %collective-permute-done.2.refs_4_.refs_7_ = bf16[256,768]{1,0:T(8,128)(2,1)S(1)} collective-permute-done((bf16[256,768]{1,0:T(8,128)(2,1)S(1)}, bf16[256,768]{1,0:T(8,128)(2,1)S(1)}, u32[]{:S(2)}, u32[]{:S(2)}) %collective-permute-start.2) | collective-permute-done | bytes 393248 | tf_op jit(solution)/shard_map/rows_second/ppermute | solution.py:371
  94.9 2.7 %collective-permute-start.5 = (bf16[256,768]{1,0:T(8,128)(2,1)S(1)}, bf16[256,768]{1,0:T(8,128)(2,1)S(1)}, u32[]{:S(2)}, u32[]{:S(2)}) collective-permute-start(bf16[256,768]{1,0:T(8,128)(2,1)S(1)} %collective-permute-done.4.refs_5_.refs_8_), channel_id=1, source_target_pairs={{0,6},{1,7},{2,0},{3,1},{4,2},{5,3},{6,4},{7,5},{8,14},{9,15},{10,... | collective-permute-start | bytes 1179656 | tf_op jit(solution)/shard_map/rows_second/ppermute | solution.py:371
  97.6 2.8 %collective-permute-start.14 = (bf16[256,768]{1,0:T(8,128)(2,1)S(1)}, bf16[256,768]{1,0:T(8,128)(2,1)S(1)}, u32[]{:S(2)}, u32[]{:S(2)}) collective-permute-start(bf16[256,768]{1,0:T(8,128)(2,1)S(1)} %collective-permute-done.1.refs_2_.refs_5_), channel_id=1, source_target_pairs={{0,1},{1,0},{2,3},{3,2},{4,5},{5,4},{6,7},{7,6},{8,9},{9,8},{10,11... | collective-permute-start | bytes 1179656 | tf_op jit(solution)/shard_map/rows_second/ppermute | solution.py:371
  100.5 2.6 %collective-permute-done.6.refs_7_.refs_10_ = bf16[256,768]{1,0:T(8,128)(2,1)S(1)} collective-permute-done((bf16[256,768]{1,0:T(8,128)(2,1)S(1)}, bf16[256,768]{1,0:T(8,128)(2,1)S(1)}, u32[]{:S(2)}, u32[]{:S(2)}) %collective-permute-start.6) | collective-permute-done | bytes 393248 | tf_op jit(solution)/shard_map/rows_second/ppermute | solution.py:371
  103.1 2.8 %collective-permute-start.17 = (bf16[256,768]{1,0:T(8,128)(2,1)S(1)}, bf16[256,768]{1,0:T(8,128)(2,1)S(1)}, u32[]{:S(2)}, u32[]{:S(2)}) collective-permute-start(bf16[256,768]{1,0:T(8,128)(2,1)S(1)} %collective-permute-done.4.refs_5_.refs_8_), channel_id=1, source_target_pairs={{0,1},{1,0},{2,3},{3,2},{4,5},{5,4},{6,7},{7,6},{8,9},{9,8},{10,11... | collective-permute-start | bytes 1179656 | tf_op jit(solution)/shard_map/rows_second/ppermute | solution.py:371
  106.1 1.7 collective-permute-start.15
  108.3 3.0 %collective-permute-start.9 = (bf16[80,768]{1,0:T(8,128)(2,1)S(1)}, bf16[80,768]{1,0:T(8,128)(2,1)}, u32[]{:S(2)}, u32[]{:S(2)}) collective-permute-start(bf16[80,768]{1,0:T(8,128)(2,1)S(1)} %slice.14), channel_id=1, source_target_pairs={{0,6},{1,7},{2,0},{3,1},{4,2},{5,3},{6,4},{7,5},{8,14},{9,15},{10,... | collective-permute-start | bytes 368648 | tf_op jit(solution)/shard_map/rows_second/ppermute | solution.py:371
  111.4 0.9 collective-permute-start.7
  112.3 1.6 collective-permute-done.9.refs_10_.refs_13_
  113.9 1.1 collective-permute-start.21
  115.4 3.5 %collective-permute-start.20 = (bf16[96,768]{1,0:T(8,128)(2,1)S(1)}, bf16[96,768]{1,0:T(8,128)(2,1)}, u32[]{:S(2)}, u32[]{:S(2)}) collective-permute-start(bf16[96,768]{1,0:T(8,128)(2,1)S(1)} %collective-permute-done.7.refs_8_.refs_11_), channel_id=1, source_target_pairs={{0,1},{1,0},{2,3},{3,2},{4,5},{5,4},{6,7},{7,6},{8,9},{9,8},{10,11... | collective-permute-start | bytes 442376 | tf_op jit(solution)/shard_map/rows_second/ppermute | solution.py:371
  118.9 0.7 copy-done.20
  119.7 3.5 %pick.1 = (bf16[512,768]{1,0:T(8,128)(2,1)}, bf16[256,768]{1,0:T(8,128)(2,1)}, bf16[256,768]{1,0:T(8,128)(2,1)}, bf16[256,768]{1,0:T(8,128)(2,1)}) custom-call(s32[4]{0:T(128)} %pad_add_fusion.refs_0_.spot_ref, bf16[256,768]{1,0:T(8,128)(2,1)} %copy-done, bf16[256,768]{1,0:T(8,128)(2,1)} %copy-done.7, bf16[256,768]{1,0:T(8,128)(2,1)} %copy-done.2, ...), custom_call_target="tpu_custom_call" | custom-call | bytes 3932160 | tf_op jit(solution)/shard_map/hessian_rows/pick/pallas_call | solution.py:228
  123.2 1.3 collective-permute-start.10
  124.4 2.5 %collective-permute-start.11 = (bf16[256,768]{1,0:T(8,128)(2,1)}, bf16[256,768]{1,0:T(8,128)(2,1)S(1)}, u32[]{:S(2)}, u32[]{:S(2)}) collective-permute-start(bf16[256,768]{1,0:T(8,128)(2,1)} %get-tuple-element.15), channel_id=1, source_target_pairs={{0,64},{32,96},{64,0},{96,32},{1,65},{33,97},{65,1},{97,33},{2,66}... | collective-permute-start | bytes 1179656 | tf_op jit(solution)/shard_map/hessian_rows/ppermute | solution.py:356
  126.9 1.1 collective-permute-start.12
  128.1 14.2 %layer.3 = (bf16[256,768]{1,0:T(8,128)(2,1)}, f32[8,256]{1,0:T(8,128)}) custom-call(s32[4]{0:T(128)} %pad_add_fusion.refs_0_.spot_ref, bf16[3,12288,256]{2,1,0:T(8,128)(2,1)} %build_dense.1.refs_1_, f32[16,1,768]{2,1,0:T(1,128)} %copy-done.10, bf16[256,768]{1,0:T(8,128)(2,1)} %copy-done, bf16[256,768]{1,0:T(8,128)(2,1)} %copy-done, ...), custom_call_target="tpu_custom_call" | custom-call | flops 4831838208 | bytes 25165824 | tf_op jit(solution)/shard_map/layer_second/layer/pallas_call | solution.py:169
  142.3 2.0 %collective-permute-done.11.refs_1_ = bf16[256,768]{1,0:T(8,128)(2,1)S(1)} collective-permute-done((bf16[256,768]{1,0:T(8,128)(2,1)}, bf16[256,768]{1,0:T(8,128)(2,1)S(1)}, u32[]{:S(2)}, u32[]{:S(2)}) %collective-permute-start.11) | collective-permute-done | bytes 393248 | tf_op jit(solution)/shard_map/hessian_rows/ppermute | solution.py:356
  144.3 0.7 copy-done.14
  145.2 0.9 collective-permute-start.28
  146.1 1.1 collective-permute-start.29
  147.2 2.8 %collective-permute-start.30 = (f32[8,256]{1,0:T(8,128)}, f32[8,256]{1,0:T(8,128)S(1)}, u32[]{:S(2)}, u32[]{:S(2)}) collective-permute-start(f32[8,256]{1,0:T(8,128)} %get-tuple-element.17.refs_3_.refs_14_), channel_id=1, source_target_pairs={{0,64},{32,96},{64,0},{96,32},{1,65},{33,97},{65,1},{97,33},{2,66}... | collective-permute-start | bytes 24584 | tf_op jit(solution)/shard_map/layer_second/ppermute | solution.py:356
  150.2 2.7 %collective-permute-start.23 = (bf16[512,768]{1,0:T(8,128)(2,1)}, bf16[512,768]{1,0:T(8,128)(2,1)S(1)}, u32[]{:S(2)}, u32[]{:S(2)}) collective-permute-start(bf16[512,768]{1,0:T(8,128)(2,1)} %get-tuple-element.13.refs_0_), channel_id=1, source_target_pairs={{0,1},{1,0},{2,3},{3,2},{4,5},{5,4},{6,7},{7,6},{8,9},{9,8},{10,11... | collective-permute-start | bytes 2359304 | tf_op jit(solution)/shard_map/hessian/ppermute | solution.py:371
  152.9 0.8 collective-permute-start.32
  153.7 1.6 collective-permute-start.24
  155.4 1.6 collective-permute-start.25
  157.0 6.8 %collective-permute-done.27.refs_8_ = bf16[256,768]{1,0:T(8,128)(2,1)S(1)} collective-permute-done((bf16[256,768]{1,0:T(8,128)(2,1)}, bf16[256,768]{1,0:T(8,128)(2,1)S(1)}, u32[]{:S(2)}, u32[]{:S(2)}) %collective-permute-start.27) | collective-permute-done | bytes 393248 | tf_op jit(solution)/shard_map/hessian/ppermute | solution.py:381
  163.8 0.9 collective-permute-start.26
  164.6 1.3 collective-permute-start.34
  166.5 0.8 broadcast_select_fusion
  167.5 0.9 collective-permute-done.33.refs_11_
  168.5 0.8 copy-done.32
  169.3 15.1 %gram.1 = f32[3072,768]{1,0:T(8,128)} custom-call(s32[4]{0:T(128)} %pad_add_fusion.refs_0_.spot_ref, bf16[512,768]{1,0:T(8,128)(2,1)} %get-tuple-element.13.refs_0_, bf16[256,768]{1,0:T(8,128)(2,1)} %get-tuple-element.18.refs_1_, bf16[256,768]{1,0:T(8,128)(2,1)} %get-tuple-element.19.refs_2_, bf16[256,768]{1,0:T(8,128)(2,1)} %get-tuple-element.20.refs_3_, ...), custom_call_target="tpu_custom_call" | custom-call | flops 4831838208 | bytes 17301504 | tf_op jit(solution)/shard_map/hessian/gram/pallas_call | solution.py:332
  (115 shorter events, 4.2 us)
Async XLA Ops:
  7.2 23.9 %copy-start.24 = (s32[1,12,48]{2,0,1:T(1,128)S(1)}, s32[1,12,48]{2,0,1:T(1,128)}, u32[]{:S(2)}) copy-start(s32[1,12,48]{2,0,1:T(1,128)} %param.7) | copy-start | bytes 6916
  7.2 48.6 %all-gather.4.cloned.1.call-start = ((), (), s32[]{:S(2)}) async-start(), calls=%async_computation.1 | async-start | bytes 6684672 | tf_op jit(solution)/shard_map/rows_first/all_gather | solution.py:415
  9.3 36.3 %all-to-all-start = ((f32[16,1,768]{2,1,0:T(1,128)}), f32[16,1,768]{2,1,0:T(1,128)S(1)}, u32[]{:S(2)}, u32[]{:S(2)}) async-start(f32[16,1,768]{2,1,0:T(1,128)} %broadcast_in_dim.13), calls=%async_computation | async-start | bytes 98304 | tf_op jit(solution)/shard_map/gains/all_to_all | solution.py:417
  16.6 103.0 %all-gather.6.cloned.1.call-start = ((), (), s32[]{:S(2)}) async-start(), calls=%async_computation.2 | async-start | bytes 1966080 | tf_op jit(solution)/shard_map/columns/all_gather | solution.py:429
  45.5 37.2 %copy-start.1 = (bf16[4,64,768]{2,1,0:T(8,128)(2,1)S(1)}, bf16[4,64,768]{2,1,0:T(8,128)(2,1)}, u32[]{:S(2)}) copy-start(bf16[4,64,768]{2,1,0:T(8,128)(2,1)} %param.4) | copy-start | bytes 1179652
  69.7 13.1 %collective-permute-start = (bf16[256,768]{1,0:T(8,128)(2,1)}, bf16[256,768]{1,0:T(8,128)(2,1)S(1)}, u32[]{:S(2)}, u32[]{:S(2)}) collective-permute-start(bf16[256,768]{1,0:T(8,128)(2,1)} %get-tuple-element.12), channel_id=1, source_target_pairs={{0,16},{1,17},{2,18},{3,19},{4,20},{5,21},{6,22},{7,23},{8,24},{9,... | collective-permute-start | bytes 1179656 | tf_op jit(solution)/shard_map/hand_over/ppermute | solution.py:426
  83.6 36.0 %copy-start = (bf16[256,768]{1,0:T(8,128)(2,1)}, bf16[256,768]{1,0:T(8,128)(2,1)S(1)}, u32[]{:S(2)}) copy-start(bf16[256,768]{1,0:T(8,128)(2,1)S(1)} %get-tuple-element.23.refs_1_.refs_3_.refs_4_) | copy-start | bytes 1179652
  83.6 10.8 %collective-permute-start.2 = (bf16[256,768]{1,0:T(8,128)(2,1)S(1)}, bf16[256,768]{1,0:T(8,128)(2,1)S(1)}, u32[]{:S(2)}, u32[]{:S(2)}) collective-permute-start(bf16[256,768]{1,0:T(8,128)(2,1)S(1)} %get-tuple-element.23.refs_1_.refs_3_.refs_4_), channel_id=1, source_target_pairs={{0,2},{1,3},{2,4},{3,5},{4,6},{5,7},{6,0},{7,1},{8,10},{9,11},{10,... | collective-permute-start | bytes 1179656 | tf_op jit(solution)/shard_map/rows_second/ppermute | solution.py:371
  84.9 10.0 %collective-permute-start.4 = (bf16[256,768]{1,0:T(8,128)(2,1)S(1)}, bf16[256,768]{1,0:T(8,128)(2,1)S(1)}, u32[]{:S(2)}, u32[]{:S(2)}) collective-permute-start(bf16[256,768]{1,0:T(8,128)(2,1)S(1)} %get-tuple-element.23.refs_1_.refs_3_.refs_4_), channel_id=1, source_target_pairs={{0,8},{1,9},{2,10},{3,11},{4,12},{5,13},{6,14},{7,15},{8,0},{9,1},... | collective-permute-start | bytes 1179656 | tf_op jit(solution)/shard_map/rows_second/ppermute | solution.py:371
  85.3 12.2 %collective-permute-start.1 = (bf16[256,768]{1,0:T(8,128)(2,1)S(1)}, bf16[256,768]{1,0:T(8,128)(2,1)S(1)}, u32[]{:S(2)}, u32[]{:S(2)}) collective-permute-start(bf16[256,768]{1,0:T(8,128)(2,1)S(1)} %get-tuple-element.23.refs_1_.refs_3_.refs_4_), channel_id=1, source_target_pairs={{0,6},{1,7},{2,0},{3,1},{4,2},{5,3},{6,4},{7,5},{8,14},{9,15},{10,... | collective-permute-start | bytes 1179656 | tf_op jit(solution)/shard_map/rows_second/ppermute | solution.py:371
  86.8 13.6 %collective-permute-start.13 = (bf16[256,768]{1,0:T(8,128)(2,1)S(1)}, bf16[256,768]{1,0:T(8,128)(2,1)S(1)}, u32[]{:S(2)}, u32[]{:S(2)}) collective-permute-start(bf16[256,768]{1,0:T(8,128)(2,1)S(1)} %get-tuple-element.23.refs_1_.refs_3_.refs_4_), channel_id=1, source_target_pairs={{0,1},{1,0},{2,3},{3,2},{4,5},{5,4},{6,7},{7,6},{8,9},{9,8},{10,11... | collective-permute-start | bytes 1179656 | tf_op jit(solution)/shard_map/rows_second/ppermute | solution.py:371
  94.4 25.2 %copy-start.5 = (bf16[256,768]{1,0:T(8,128)(2,1)}, bf16[256,768]{1,0:T(8,128)(2,1)S(1)}, u32[]{:S(2)}) copy-start(bf16[256,768]{1,0:T(8,128)(2,1)S(1)} %collective-permute-done.2.refs_4_.refs_7_) | copy-start | bytes 1179652
  94.4 8.7 %collective-permute-start.6 = (bf16[256,768]{1,0:T(8,128)(2,1)S(1)}, bf16[256,768]{1,0:T(8,128)(2,1)S(1)}, u32[]{:S(2)}, u32[]{:S(2)}) collective-permute-start(bf16[256,768]{1,0:T(8,128)(2,1)S(1)} %collective-permute-done.2.refs_4_.refs_7_), channel_id=1, source_target_pairs={{0,8},{1,9},{2,10},{3,11},{4,12},{5,13},{6,14},{7,15},{8,0},{9,1},... | collective-permute-start | bytes 1179656 | tf_op jit(solution)/shard_map/rows_second/ppermute | solution.py:371
  94.9 11.1 %collective-permute-start.3 = (bf16[256,768]{1,0:T(8,128)(2,1)S(1)}, bf16[256,768]{1,0:T(8,128)(2,1)S(1)}, u32[]{:S(2)}, u32[]{:S(2)}) collective-permute-start(bf16[256,768]{1,0:T(8,128)(2,1)S(1)} %collective-permute-done.2.refs_4_.refs_7_), channel_id=1, source_target_pairs={{0,2},{1,3},{2,4},{3,5},{4,6},{5,7},{6,0},{7,1},{8,10},{9,11},{10,... | collective-permute-start | bytes 1179656 | tf_op jit(solution)/shard_map/rows_second/ppermute | solution.py:371
  94.9 24.7 %copy-start.6 = (bf16[256,768]{1,0:T(8,128)(2,1)}, bf16[256,768]{1,0:T(8,128)(2,1)S(1)}, u32[]{:S(2)}) copy-start(bf16[256,768]{1,0:T(8,128)(2,1)S(1)} %collective-permute-done.4.refs_5_.refs_8_) | copy-start | bytes 1179652
  94.9 11.1 %collective-permute-start.5 = (bf16[256,768]{1,0:T(8,128)(2,1)S(1)}, bf16[256,768]{1,0:T(8,128)(2,1)S(1)}, u32[]{:S(2)}, u32[]{:S(2)}) collective-permute-start(bf16[256,768]{1,0:T(8,128)(2,1)S(1)} %collective-permute-done.4.refs_5_.refs_8_), channel_id=1, source_target_pairs={{0,6},{1,7},{2,0},{3,1},{4,2},{5,3},{6,4},{7,5},{8,14},{9,15},{10,... | collective-permute-start | bytes 1179656 | tf_op jit(solution)/shard_map/rows_second/ppermute | solution.py:371
  97.6 22.0 %copy-start.7 = (bf16[256,768]{1,0:T(8,128)(2,1)}, bf16[256,768]{1,0:T(8,128)(2,1)S(1)}, u32[]{:S(2)}) copy-start(bf16[256,768]{1,0:T(8,128)(2,1)S(1)} %collective-permute-done.1.refs_2_.refs_5_) | copy-start | bytes 1179652
  97.6 10.2 %collective-permute-start.14 = (bf16[256,768]{1,0:T(8,128)(2,1)S(1)}, bf16[256,768]{1,0:T(8,128)(2,1)S(1)}, u32[]{:S(2)}, u32[]{:S(2)}) collective-permute-start(bf16[256,768]{1,0:T(8,128)(2,1)S(1)} %collective-permute-done.1.refs_2_.refs_5_), channel_id=1, source_target_pairs={{0,1},{1,0},{2,3},{3,2},{4,5},{5,4},{6,7},{7,6},{8,9},{9,8},{10,11... | collective-permute-start | bytes 1179656 | tf_op jit(solution)/shard_map/rows_second/ppermute | solution.py:371
  100.4 7.4 %collective-permute-start.16 = (bf16[256,768]{1,0:T(8,128)(2,1)S(1)}, bf16[256,768]{1,0:T(8,128)(2,1)S(1)}, u32[]{:S(2)}, u32[]{:S(2)}) collective-permute-start(bf16[256,768]{1,0:T(8,128)(2,1)S(1)} %collective-permute-done.2.refs_4_.refs_7_), channel_id=1, source_target_pairs={{0,1},{1,0},{2,3},{3,2},{4,5},{5,4},{6,7},{7,6},{8,9},{9,8},{10,11... | collective-permute-start | bytes 1179656 | tf_op jit(solution)/shard_map/rows_second/ppermute | solution.py:371
  103.1 16.5 %copy-start.3 = (bf16[256,768]{1,0:T(8,128)(2,1)}, bf16[256,768]{1,0:T(8,128)(2,1)S(1)}, u32[]{:S(2)}) copy-start(bf16[256,768]{1,0:T(8,128)(2,1)S(1)} %collective-permute-done.6.refs_7_.refs_10_) | copy-start | bytes 1179652
  103.1 5.2 %collective-permute-start.17 = (bf16[256,768]{1,0:T(8,128)(2,1)S(1)}, bf16[256,768]{1,0:T(8,128)(2,1)S(1)}, u32[]{:S(2)}, u32[]{:S(2)}) collective-permute-start(bf16[256,768]{1,0:T(8,128)(2,1)S(1)} %collective-permute-done.4.refs_5_.refs_8_), channel_id=1, source_target_pairs={{0,1},{1,0},{2,3},{3,2},{4,5},{5,4},{6,7},{7,6},{8,9},{9,8},{10,11... | collective-permute-start | bytes 1179656 | tf_op jit(solution)/shard_map/rows_second/ppermute | solution.py:371
  106.0 13.7 %copy-start.2 = (bf16[256,768]{1,0:T(8,128)(2,1)}, bf16[256,768]{1,0:T(8,128)(2,1)S(1)}, u32[]{:S(2)}) copy-start(bf16[256,768]{1,0:T(8,128)(2,1)S(1)} %collective-permute-done.3.refs_3_.refs_6_) | copy-start | bytes 1179652
  106.0 5.4 %collective-permute-start.8 = (bf16[80,768]{1,0:T(8,128)(2,1)S(1)}, bf16[80,768]{1,0:T(8,128)(2,1)S(1)}, u32[]{:S(2)}, u32[]{:S(2)}) collective-permute-start(bf16[80,768]{1,0:T(8,128)(2,1)S(1)} %slice.13), channel_id=1, source_target_pairs={{0,2},{1,3},{2,4},{3,5},{4,6},{5,7},{6,0},{7,1},{8,10},{9,11},{10,... | collective-permute-start | bytes 368648 | tf_op jit(solution)/shard_map/rows_second/ppermute | solution.py:371
  106.1 20.9 %collective-permute-start.15 = (bf16[256,768]{1,0:T(8,128)(2,1)S(1)}, bf16[256,768]{1,0:T(8,128)(2,1)}, u32[]{:S(2)}, u32[]{:S(2)}) collective-permute-start(bf16[256,768]{1,0:T(8,128)(2,1)S(1)} %collective-permute-done.3.refs_3_.refs_6_), channel_id=1, source_target_pairs={{0,1},{1,0},{2,3},{3,2},{4,5},{5,4},{6,7},{7,6},{8,9},{9,8},{10,11... | collective-permute-start | bytes 1179656 | tf_op jit(solution)/shard_map/rows_second/ppermute | solution.py:371
  107.7 20.3 %collective-permute-start.18 = (bf16[256,768]{1,0:T(8,128)(2,1)S(1)}, bf16[256,768]{1,0:T(8,128)(2,1)}, u32[]{:S(2)}, u32[]{:S(2)}) collective-permute-start(bf16[256,768]{1,0:T(8,128)(2,1)S(1)} %collective-permute-done.5.refs_6_.refs_9_), channel_id=1, source_target_pairs={{0,1},{1,0},{2,3},{3,2},{4,5},{5,4},{6,7},{7,6},{8,9},{9,8},{10,11... | collective-permute-start | bytes 1179656 | tf_op jit(solution)/shard_map/rows_second/ppermute | solution.py:371
  107.9 20.2 %collective-permute-start.19 = (bf16[256,768]{1,0:T(8,128)(2,1)S(1)}, bf16[256,768]{1,0:T(8,128)(2,1)}, u32[]{:S(2)}, u32[]{:S(2)}) collective-permute-start(bf16[256,768]{1,0:T(8,128)(2,1)S(1)} %collective-permute-done.6.refs_7_.refs_10_), channel_id=1, source_target_pairs={{0,1},{1,0},{2,3},{3,2},{4,5},{5,4},{6,7},{7,6},{8,9},{9,8},{10,11... | collective-permute-start | bytes 1179656 | tf_op jit(solution)/shard_map/rows_second/ppermute | solution.py:371
  108.3 5.6 %collective-permute-start.9 = (bf16[80,768]{1,0:T(8,128)(2,1)S(1)}, bf16[80,768]{1,0:T(8,128)(2,1)}, u32[]{:S(2)}, u32[]{:S(2)}) collective-permute-start(bf16[80,768]{1,0:T(8,128)(2,1)S(1)} %slice.14), channel_id=1, source_target_pairs={{0,6},{1,7},{2,0},{3,1},{4,2},{5,3},{6,4},{7,5},{8,14},{9,15},{10,... | collective-permute-start | bytes 368648 | tf_op jit(solution)/shard_map/rows_second/ppermute | solution.py:371
  111.4 4.0 %collective-permute-start.7 = (bf16[96,768]{1,0:T(8,128)(2,1)S(1)}, bf16[96,768]{1,0:T(8,128)(2,1)S(1)}, u32[]{:S(2)}, u32[]{:S(2)}) collective-permute-start(bf16[96,768]{1,0:T(8,128)(2,1)S(1)} %slice.12), channel_id=1, source_target_pairs={{0,8},{1,9},{2,10},{3,11},{4,12},{5,13},{6,14},{7,15},{8,0},{9,1},... | collective-permute-start | bytes 442376 | tf_op jit(solution)/shard_map/rows_second/ppermute | solution.py:371
  113.9 5.0 %collective-permute-start.21 = (bf16[80,768]{1,0:T(8,128)(2,1)S(1)}, bf16[80,768]{1,0:T(8,128)(2,1)S(1)}, u32[]{:S(2)}, u32[]{:S(2)}) collective-permute-start(bf16[80,768]{1,0:T(8,128)(2,1)S(1)} %collective-permute-done.8.refs_9_.refs_12_), channel_id=1, source_target_pairs={{0,1},{1,0},{2,3},{3,2},{4,5},{5,4},{6,7},{7,6},{8,9},{9,8},{10,11... | collective-permute-start | bytes 368648 | tf_op jit(solution)/shard_map/rows_second/ppermute | solution.py:371
  115.4 9.1 %collective-permute-start.20 = (bf16[96,768]{1,0:T(8,128)(2,1)S(1)}, bf16[96,768]{1,0:T(8,128)(2,1)}, u32[]{:S(2)}, u32[]{:S(2)}) collective-permute-start(bf16[96,768]{1,0:T(8,128)(2,1)S(1)} %collective-permute-done.7.refs_8_.refs_11_), channel_id=1, source_target_pairs={{0,1},{1,0},{2,3},{3,2},{4,5},{5,4},{6,7},{7,6},{8,9},{9,8},{10,11... | collective-permute-start | bytes 442376 | tf_op jit(solution)/shard_map/rows_second/ppermute | solution.py:371
  119.6 3.6 %collective-permute-start.22 = (bf16[80,768]{1,0:T(8,128)(2,1)}, bf16[80,768]{1,0:T(8,128)(2,1)}, u32[]{:S(2)}, u32[]{:S(2)}) collective-permute-start(bf16[80,768]{1,0:T(8,128)(2,1)} %collective-permute-done.9.refs_10_.refs_13_), channel_id=1, source_target_pairs={{0,1},{1,0},{2,3},{3,2},{4,5},{5,4},{6,7},{7,6},{8,9},{9,8},{10,11... | collective-permute-start | bytes 368648 | tf_op jit(solution)/shard_map/rows_second/ppermute | solution.py:371
  123.2 19.1 %collective-permute-start.10 = (bf16[256,768]{1,0:T(8,128)(2,1)}, bf16[256,768]{1,0:T(8,128)(2,1)S(1)}, u32[]{:S(2)}, u32[]{:S(2)}) collective-permute-start(bf16[256,768]{1,0:T(8,128)(2,1)} %get-tuple-element.14), channel_id=1, source_target_pairs={{0,32},{32,64},{64,96},{96,0},{1,33},{33,65},{65,97},{97,1},{2,34}... | collective-permute-start | bytes 1179656 | tf_op jit(solution)/shard_map/hessian_rows/ppermute | solution.py:356
  124.4 19.9 %collective-permute-start.11 = (bf16[256,768]{1,0:T(8,128)(2,1)}, bf16[256,768]{1,0:T(8,128)(2,1)S(1)}, u32[]{:S(2)}, u32[]{:S(2)}) collective-permute-start(bf16[256,768]{1,0:T(8,128)(2,1)} %get-tuple-element.15), channel_id=1, source_target_pairs={{0,64},{32,96},{64,0},{96,32},{1,65},{33,97},{65,1},{97,33},{2,66}... | collective-permute-start | bytes 1179656 | tf_op jit(solution)/shard_map/hessian_rows/ppermute | solution.py:356
  126.9 39.5 %copy-start.12 = (bf16[256,768]{1,0:T(8,128)(2,1)S(1)}, bf16[256,768]{1,0:T(8,128)(2,1)}, u32[]{:S(2)}) copy-start(bf16[256,768]{1,0:T(8,128)(2,1)} %get-tuple-element.12) | copy-start | bytes 1179652
  126.9 17.4 %collective-permute-start.12 = (bf16[256,768]{1,0:T(8,128)(2,1)}, bf16[256,768]{1,0:T(8,128)(2,1)S(1)}, u32[]{:S(2)}, u32[]{:S(2)}) collective-permute-start(bf16[256,768]{1,0:T(8,128)(2,1)} %get-tuple-element.16), channel_id=1, source_target_pairs={{0,96},{32,0},{64,32},{96,64},{1,97},{33,1},{65,33},{97,65},{2,98}... | collective-permute-start | bytes 1179656 | tf_op jit(solution)/shard_map/hessian_rows/ppermute | solution.py:356
  145.2 10.1 %collective-permute-start.28 = (bf16[256,768]{1,0:T(8,128)(2,1)}, bf16[256,768]{1,0:T(8,128)(2,1)S(1)}, u32[]{:S(2)}, u32[]{:S(2)}) collective-permute-start(bf16[256,768]{1,0:T(8,128)(2,1)} %get-tuple-element.19.refs_2_), channel_id=1, source_target_pairs={{0,8},{1,9},{2,10},{3,11},{4,12},{5,13},{6,14},{7,15},{8,0},{9,1},... | collective-permute-start | bytes 1179656 | tf_op jit(solution)/shard_map/hessian/ppermute | solution.py:381
  146.1 6.8 %collective-permute-start.29 = (f32[8,256]{1,0:T(8,128)}, f32[8,256]{1,0:T(8,128)S(1)}, u32[]{:S(2)}, u32[]{:S(2)}) collective-permute-start(f32[8,256]{1,0:T(8,128)} %get-tuple-element.17.refs_3_.refs_14_), channel_id=1, source_target_pairs={{0,32},{32,64},{64,96},{96,0},{1,33},{33,65},{65,97},{97,1},{2,34}... | collective-permute-start | bytes 24584 | tf_op jit(solution)/shard_map/layer_second/ppermute | solution.py:356
  147.2 5.6 %collective-permute-start.30 = (f32[8,256]{1,0:T(8,128)}, f32[8,256]{1,0:T(8,128)S(1)}, u32[]{:S(2)}, u32[]{:S(2)}) collective-permute-start(f32[8,256]{1,0:T(8,128)} %get-tuple-element.17.refs_3_.refs_14_), channel_id=1, source_target_pairs={{0,64},{32,96},{64,0},{96,32},{1,65},{33,97},{65,1},{97,33},{2,66}... | collective-permute-start | bytes 24584 | tf_op jit(solution)/shard_map/layer_second/ppermute | solution.py:356
  150.0 3.7 %collective-permute-start.31 = (f32[8,256]{1,0:T(8,128)}, f32[8,256]{1,0:T(8,128)S(1)}, u32[]{:S(2)}, u32[]{:S(2)}) collective-permute-start(f32[8,256]{1,0:T(8,128)} %get-tuple-element.17.refs_3_.refs_14_), channel_id=1, source_target_pairs={{0,96},{32,0},{64,32},{96,64},{1,97},{33,1},{65,33},{97,65},{2,98}... | collective-permute-start | bytes 24584 | tf_op jit(solution)/shard_map/layer_second/ppermute | solution.py:356
  150.2 17.1 %collective-permute-start.23 = (bf16[512,768]{1,0:T(8,128)(2,1)}, bf16[512,768]{1,0:T(8,128)(2,1)S(1)}, u32[]{:S(2)}, u32[]{:S(2)}) collective-permute-start(bf16[512,768]{1,0:T(8,128)(2,1)} %get-tuple-element.13.refs_0_), channel_id=1, source_target_pairs={{0,1},{1,0},{2,3},{3,2},{4,5},{5,4},{6,7},{7,6},{8,9},{9,8},{10,11... | collective-permute-start | bytes 2359304 | tf_op jit(solution)/shard_map/hessian/ppermute | solution.py:371
  152.9 10.9 %collective-permute-start.27 = (bf16[256,768]{1,0:T(8,128)(2,1)}, bf16[256,768]{1,0:T(8,128)(2,1)S(1)}, u32[]{:S(2)}, u32[]{:S(2)}) collective-permute-start(bf16[256,768]{1,0:T(8,128)(2,1)} %get-tuple-element.18.refs_1_), channel_id=1, source_target_pairs={{0,2},{1,3},{2,0},{3,1},{4,6},{5,7},{6,4},{7,5},{8,10},{9,11},{10,... | collective-permute-start | bytes 1179656 | tf_op jit(solution)/shard_map/hessian/ppermute | solution.py:381
  152.9 11.7 %collective-permute-start.32 = (bf16[256,768]{1,0:T(8,128)(2,1)}, bf16[256,768]{1,0:T(8,128)(2,1)S(1)}, u32[]{:S(2)}, u32[]{:S(2)}) collective-permute-start(bf16[256,768]{1,0:T(8,128)(2,1)} %get-tuple-element.20.refs_3_), channel_id=1, source_target_pairs={{0,6},{1,7},{2,4},{3,5},{4,2},{5,3},{6,0},{7,1},{8,14},{9,15},{10,... | collective-permute-start | bytes 1179656 | tf_op jit(solution)/shard_map/hessian/ppermute | solution.py:381
  153.7 12.2 %collective-permute-start.24 = (bf16[256,768]{1,0:T(8,128)(2,1)}, bf16[256,768]{1,0:T(8,128)(2,1)S(1)}, u32[]{:S(2)}, u32[]{:S(2)}) collective-permute-start(bf16[256,768]{1,0:T(8,128)(2,1)} %get-tuple-element.18.refs_1_), channel_id=1, source_target_pairs={{0,1},{1,0},{2,3},{3,2},{4,5},{5,4},{6,7},{7,6},{8,9},{9,8},{10,11... | collective-permute-start | bytes 1179656 | tf_op jit(solution)/shard_map/hessian/ppermute | solution.py:371
  155.4 10.7 %collective-permute-start.25 = (bf16[256,768]{1,0:T(8,128)(2,1)}, bf16[256,768]{1,0:T(8,128)(2,1)S(1)}, u32[]{:S(2)}, u32[]{:S(2)}) collective-permute-start(bf16[256,768]{1,0:T(8,128)(2,1)} %get-tuple-element.19.refs_2_), channel_id=1, source_target_pairs={{0,1},{1,0},{2,3},{3,2},{4,5},{5,4},{6,7},{7,6},{8,9},{9,8},{10,11... | collective-permute-start | bytes 1179656 | tf_op jit(solution)/shard_map/hessian/ppermute | solution.py:371
  163.8 3.5 %collective-permute-start.26 = (bf16[256,768]{1,0:T(8,128)(2,1)}, bf16[256,768]{1,0:T(8,128)(2,1)S(1)}, u32[]{:S(2)}, u32[]{:S(2)}) collective-permute-start(bf16[256,768]{1,0:T(8,128)(2,1)} %get-tuple-element.20.refs_3_), channel_id=1, source_target_pairs={{0,1},{1,0},{2,3},{3,2},{4,5},{5,4},{6,7},{7,6},{8,9},{9,8},{10,11... | collective-permute-start | bytes 1179656 | tf_op jit(solution)/shard_map/hessian/ppermute | solution.py:371
  164.6 2.9 %collective-permute-start.34 = (bf16[256,768]{1,0:T(8,128)(2,1)}, bf16[256,768]{1,0:T(8,128)(2,1)S(1)}, u32[]{:S(2)}, u32[]{:S(2)}) collective-permute-start(bf16[256,768]{1,0:T(8,128)(2,1)} %after.3.refs_9_), channel_id=1, source_target_pairs={{0,1},{1,0},{2,3},{3,2},{4,5},{5,4},{6,7},{7,6},{8,9},{9,8},{10,11... | collective-permute-start | bytes 1179656 | tf_op jit(solution)/shard_map/hessian/ppermute | solution.py:371
  165.9 2.5 %collective-permute-start.33 = (bf16[256,768]{1,0:T(8,128)(2,1)S(1)}, bf16[256,768]{1,0:T(8,128)(2,1)S(1)}, u32[]{:S(2)}, u32[]{:S(2)}) collective-permute-start(bf16[256,768]{1,0:T(8,128)(2,1)S(1)} %collective-permute-done.27.refs_8_), channel_id=1, source_target_pairs={{0,1},{1,0},{2,3},{3,2},{4,5},{5,4},{6,7},{7,6},{8,9},{9,8},{10,11... | collective-permute-start | bytes 1179656 | tf_op jit(solution)/shard_map/hessian/ppermute | solution.py:371
  166.0 3.2 %collective-permute-start.35 = (bf16[256,768]{1,0:T(8,128)(2,1)S(1)}, bf16[256,768]{1,0:T(8,128)(2,1)}, u32[]{:S(2)}, u32[]{:S(2)}) collective-permute-start(bf16[256,768]{1,0:T(8,128)(2,1)S(1)} %collective-permute-done.32.refs_10_), channel_id=1, source_target_pairs={{0,1},{1,0},{2,3},{3,2},{4,5},{5,4},{6,7},{7,6},{8,9},{9,8},{10,11... | collective-permute-start | bytes 1179656 | tf_op jit(solution)/shard_map/hessian/ppermute | solution.py:371
  (24 other events, 110.7 us)
Sparse Core Ops, SparseCore 0:
  9.7 46.0 all-gather.3
  83.7 28.6 all-gather.5
where the time goes:
time: 192 us; the launch traced here: 191 us
  Pallas kernels  60.5 us (32%)
  starting transfers between devices  56 us (29%)
  waiting for transfers between devices  39.7 us (21%)
  local copies, waits for them, and re-layouts  17.5 us (9%)
  between operations  14.4 us (8%)
  other arithmetic  2.99 us (2%)
    ppermute x26, starting transfers between devices, shift(): return lax.ppermute(value, 'tensor', pairs)  33.5 us
    pallas_call x2, Pallas kernels, layer(): pl.pallas_call(lambda *refs: layer_kernel(pieces, count, straight, *refs)...  28.1 us
    pallas_call x1, Pallas kernels, gram(): pl.pallas_call(gram_kernel, in_specs=[SMEM] + [ANY] * (4 * DP - 2) + [VME...  15.1 us
    pallas_call x1, Pallas kernels, build_dense(): pl.pallas_call(build_kernel, grid_spec=pltpu.PrefetchScalarGridSpec(num_s...  13.8 us
    squeeze x1, local copies, waits for them, and re-layouts, build_dense(): blocks = values.reshape(WIDTH // BLOCK, KEEP, BLOCK, BLOCK)  13.8 us
    ppermute x26, waiting for transfers between devices, shift(): return lax.ppermute(value, 'tensor', pairs)  11.5 us
    all_gather x1, waiting for transfers between devices, body(): gathered = lax.all_gather(own, 'tensor', axis=0, tiled=True)  10.2 us
    ppermute x6, starting transfers between devices, along_dp(): lax.ppermute(value, 'dp', [(source, (source + step) % DP) for source in r...  8.91 us
  transfers between devices with their start and end apart: 39, of which 11 were waited for; matrix products, arithmetic and copies ran while one was open for 9% of the time, Pallas kernels for 16%

commit v1 on v0

--- a/solution.py
+++ b/solution.py
@@ -84,6 +84,8 @@
 
 
 def layer_kernel(pieces, count, straight, spot_ref, weight_ref, gains_ref, own_ref, *refs):
+    if not straight:
+        earlier_ref, refs = refs[0], refs[1:]
     sources, (out_ref, stats_ref, rows, weight, total, means, scales, sems, weight_sems) = refs[:count], refs[count:]
 
     def place(position):
@@ -158,17 +160,22 @@
             normalise(position + 3)
 
     out_ref[...] = total[...].astype(jnp.bfloat16)
+    if not straight:
+
+        @pl.when(spot_ref[4] == 0)
+        def _():
+            out_ref[...] = earlier_ref[...]
 
 
 def in_hbm(arrays):
     return [pltpu.with_memory_space_constraint(array, pltpu.HBM) for array in arrays]
 
 
-def layer(spot, gathered, pieces, weight, gains, own, straight):
-    count = len(gathered)
+def layer(spot, gathered, pieces, weight, gains, own, earlier=None):
+    count, straight = len(gathered), earlier is None
     return pl.pallas_call(
         lambda *refs: layer_kernel(pieces, count, straight, *refs),
-        in_specs=[SMEM, ANY, VMEM, VMEM] + [ANY] * count,
+        in_specs=[SMEM, ANY, VMEM, VMEM] + [VMEM] * (not straight) + [ANY] * count,
         out_specs=[VMEM, VMEM],
         out_shape=[
             jax.ShapeDtypeStruct((ROWS, WIDTH), jnp.bfloat16),
@@ -186,7 +193,7 @@
         compiler_params=pltpu.CompilerParams(vmem_limit_bytes=VMEM_LIMIT),
         cost_estimate=pl.CostEstimate(flops=2 * ROWS * D * WIDTH, bytes_accessed=2 * D * (WIDTH + ROWS), transcendentals=ROWS),
         name="layer",
-    )(spot, *in_hbm([weight]), gains, own, *in_hbm(gathered))
+    )(spot, *in_hbm([weight]), gains, own, *([] if straight else [earlier]), *in_hbm(gathered))
 
 
 PIECE = 384
@@ -252,7 +259,7 @@
 def gram_kernel(spot_ref, *refs):
     near, far, refs = refs[:2 * DP], refs[2 * DP:4 * DP - 2], refs[4 * DP - 2:]
     stats_refs, refs = refs[:DP], refs[DP:]
-    cols_ref, gains_ref, col_gain_ref, out_ref, rows, cols, means, scales, left, result, sems, row_sems = refs
+    cols_ref, gains_ref, col_gain_ref, out_ref, rows, given, cols, means, scales, left, result, sems, row_sems, col_sem = refs
 
     def block_of(group):
         return lax.rem(spot_ref[3] + group // HALF, 2) + 2 * lax.rem(group, HALF)
@@ -268,16 +275,20 @@
             row_copy(near[side * DP + part], side * HALF + half, part).start()
             row_copy(far[side * (DP - 1) + part - 1], side * HALF + 1 - half, part).start()
 
+    columns = pltpu.make_async_copy(cols_ref, given, col_sem)
+    columns.start()
     start_rows(0)
     for part in range(DP):
         span = slice(part * ROWS, (part + 1) * ROWS)
         means[span] = jnp.transpose(jnp.broadcast_to(stats_refs[part][0:1], (LANES, ROWS)))
         scales[span] = jnp.transpose(jnp.broadcast_to(stats_refs[part][1:2], (LANES, ROWS)))
+    columns.wait()
+    for part in range(DP):
         for chunk in range(0, ROWS, CHUNK):
             span = slice(part * ROWS + chunk, part * ROWS + chunk + CHUNK)
             for lane in range(WIDTH // LANES):
                 lanes = slice(lane * LANES, (lane + 1) * LANES)
-                values = cols_ref[lax.rem(spot_ref[0] + DP - part, DP), chunk:chunk + CHUNK, lanes].astype(jnp.float32)
+                values = given[lax.rem(spot_ref[0] + DP - part, DP), chunk:chunk + CHUNK, lanes].astype(jnp.float32)
                 scaled = (values - means[span]) * scales[span] * col_gain_ref[:, lanes]
                 cols[span, lanes] = scaled.astype(jnp.bfloat16)
 
@@ -303,26 +314,19 @@
     normalise(0, 0)
     start_rows(1)
 
-    @pl.loop(0, len(CLASSES))
-    def _(group):
+    for group in range(len(CLASSES)):
         for slot in range(PER):
             product = lax.dot_general(
                 left[slot], cols[...], (((0,), (0,)), ((), ())), preferred_element_type=jnp.float32
             )
-
-            @pl.when(group > 0)
-            def _():
+            if group > 0:
                 store(group - 1, slot).wait()
-
             result[slot] = product * (2.0 / (DP * ROWS))
             store(group, slot).start()
             if slot + 1 < PER:
                 normalise(group, slot + 1)
-            else:
-
-                @pl.when(group + 1 < len(CLASSES))
-                def _():
-                    normalise(group + 1, 0)
+            elif group + 1 < len(CLASSES):
+                normalise(group + 1, 0)
 
     for slot in range(PER):
         store(len(CLASSES) - 1, slot).wait()
@@ -331,11 +335,12 @@
 def gram(spot, near, far, cols, stats, gains, col_gain):
     return pl.pallas_call(
         gram_kernel,
-        in_specs=[SMEM] + [ANY] * (4 * DP - 2) + [VMEM] * (DP + 3),
+        in_specs=[SMEM] + [ANY] * (4 * DP - 2) + [VMEM] * DP + [ANY, VMEM, VMEM],
         out_specs=ANY,
         out_shape=jax.ShapeDtypeStruct((QUARTER, WIDTH), jnp.float32),
         scratch_shapes=[
             pltpu.VMEM((len(CLASSES), DP, ROWS, WIDTH), jnp.bfloat16),
+            pltpu.VMEM((DP, ROWS, WIDTH), jnp.bfloat16),
             pltpu.VMEM((DP * ROWS, WIDTH), jnp.bfloat16),
             pltpu.VMEM((DP * ROWS, LANES), jnp.float32),
             pltpu.VMEM((DP * ROWS, LANES), jnp.float32),
@@ -343,13 +348,14 @@
             pltpu.VMEM((2, PIECE, WIDTH), jnp.float32),
             pltpu.SemaphoreType.DMA((2,)),
             pltpu.SemaphoreType.DMA((len(CLASSES), DP)),
+            pltpu.SemaphoreType.DMA(()),
         ],
         compiler_params=pltpu.CompilerParams(vmem_limit_bytes=VMEM_LIMIT),
         cost_estimate=pl.CostEstimate(
             flops=2 * DP * ROWS * QUARTER * WIDTH, bytes_accessed=4 * QUARTER * WIDTH + 2 * DP * ROWS * (QUARTER + WIDTH), transcendentals=0
         ),
         name="gram",
-    )(spot, *near, *far, *stats, cols, gains, col_gain)
+    )(spot, *near, *far, *stats, *in_hbm([cols]), gains, col_gain)
 
 
 def along_dp(value, step):
@@ -418,10 +424,10 @@
         all_gains = all_gains[:, None, :]
     with jax.named_scope("weight"):
         weight = build_dense(block_values[0], block_rows[0])
-    spot = jnp.stack([quarter, here // 8, here // 2 % 4, here % 2]).astype(jnp.int32)
+    spot = jnp.stack([quarter, here // 8, here // 2 % 4, here % 2, lax.axis_index("pipe")]).astype(jnp.int32)
     with jax.named_scope("layer_first"):
         pieces = [(0, block * ROWS, ROWS, block, 0) for block in range(TENSOR)]
-        updated_first, _ = layer(spot, [gathered], pieces, weight, all_gains, own, True)
+        updated_first, _ = layer(spot, [gathered], pieces, weight, all_gains, own)
     with jax.named_scope("hand_over"):
         received = lax.ppermute(updated_first, "pipe", [(0, 1)])
     stream = jnp.where(first, own, received)
@@ -434,7 +440,7 @@
         picked = pick(spot, arrays[:mine], [piece for piece in pieces if piece[0] < mine], cols)
         rows = [along_dp(picked[step], step) for step in range(1, DP)]
     with jax.named_scope("layer_second"):
-        updated_second, stats = layer(spot, arrays, pieces, weight, all_gains, stream, False)
+        sections, stats = layer(spot, arrays, pieces, weight, all_gains, stream, updated_first)
         stats = gather_dp(stats)
     with jax.named_scope("hessian"):
         near = [picked[0], *after(rows, [stats[0]])]
@@ -443,7 +449,6 @@
         near += [shift(value, 0, 0, 1) for value in near]
         far += [shift(value, 0, 0, 1) for value in far]
         hessian = gram(spot, near, far, cols, stats, all_gains, gain[None, :])
-    sections = jnp.where(first, updated_first, updated_second)
     return (hessian[None], sections.reshape(1, M, TOK, WIDTH))
 
 

time: 192 us -> 191 us (level)
  transfers between devices with their start and end apart: 39 -> 39, of which waited for: 11 -> 11; matrix products, arithmetic and copies ran while one was open for 9% -> 9% of each run, Pallas kernels for 16% -> 17%
where the time goes in v1:
time: 191 us; the launch traced here: 190 us
  Pallas kernels  59.3 us (31%)
  starting transfers between devices  56 us (29%)
  waiting for transfers between devices  40.5 us (21%)
  local copies, waits for them, and re-layouts  18.1 us (9%)
  between operations  14.4 us (8%)
    ppermute x26, starting transfers between devices, shift(): return lax.ppermute(value, 'tensor', pairs)  33.4 us
    pallas_call x2, Pallas kernels, layer(): pl.pallas_call(lambda *refs: layer_kernel(pieces, count, straight, *refs)...  28.3 us
    pallas_call x1, Pallas kernels, build_dense(): pl.pallas_call(build_kernel, grid_spec=pltpu.PrefetchScalarGridSpec(num_s...  13.8 us
    squeeze x1, local copies, waits for them, and re-layouts, build_dense(): blocks = values.reshape(WIDTH // BLOCK, KEEP, BLOCK, BLOCK)  13.8 us
    pallas_call x1, Pallas kernels, gram(): pl.pallas_call(gram_kernel, in_specs=[SMEM] + [ANY] * (4 * DP - 2) + [VME...  13.6 us
    ppermute x26, waiting for transfers between devices, shift(): return lax.ppermute(value, 'tensor', pairs)  12.3 us
    all_gather x1, waiting for transfers between devices, body(): gathered = lax.all_gather(own, 'tensor', axis=0, tiled=True)  10.3 us
    ppermute x6, starting transfers between devices, along_dp(): lax.ppermute(value, 'dp', [(source, (source + step) % DP) for source in r...  8.9 us
  transfers between devices with their start and end apart: 39, of which 11 were waited for; matrix products, arithmetic and copies ran while one was open for 9% of the time, Pallas kernels for 17%

profile of v1, /device:TPU:1, one launch (start us, length us, event | category | flops | bytes accessed | tf_op | source)
XLA Modules:
  0.0 189.7 jit_solution(17133890371767989113)
XLA Ops:
  7.2 0.7 all-gather.4.cloned.1.call-update
  7.9 0.7 reduce
  8.6 0.6 broadcast_in_dim.13
  9.3 7.3 %all-to-all-start = ((f32[16,1,768]{2,1,0:T(1,128)}), f32[16,1,768]{2,1,0:T(1,128)S(1)}, u32[]{:S(2)}, u32[]{:S(2)}) async-start(f32[16,1,768]{2,1,0:T(1,128)} %broadcast_in_dim.13), calls=%async_computation | async-start | bytes 98304 | tf_op jit(solution)/shard_map/gains/all_to_all | solution.py:423
  16.7 13.8 %squeeze.7.blocks_ref = bf16[12,48,64,64]{3,2,1,0:T(8,128)(2,1)} reshape(bf16[1,12,48,4096]{3,2,1,0:T(8,128)(2,1)} %param.6) | data formatting | bytes 9437184 | tf_op jit(solution)/shard_map/weight/reshape;weight/squeeze | solution.py:47
  31.1 13.8 %build_dense.1.refs_1_ = bf16[3,12288,256]{2,1,0:T(8,128)(2,1)} custom-call(s32[12,48]{1,0:T(8,128)} %bitcast.20, bf16[12,48,64,64]{3,2,1,0:T(8,128)(2,1)} %squeeze.7.blocks_ref), custom_call_target="tpu_custom_call" | custom-call | bytes 33554432 | tf_op jit(solution)/shard_map/weight/build_dense/pallas_call | solution.py:49
  44.9 0.6 stack.23.refs_0_.spot_ref
  45.5 10.3 %all-gather.4.cloned.1.call-done.refs_4_ = bf16[4096,768]{1,0:T(8,128)(2,1)} async-done(((bf16[256,768]{1,0:T(8,128)(2,1)}), bf16[4096,768]{1,0:T(8,128)(2,1)}) %all-gather.4.cloned.1.call-update) | async-done | bytes 6291472 | tf_op jit(solution)/shard_map/rows_first/all_gather | solution.py:421
  55.8 13.9 %layer.2 = (bf16[256,768]{1,0:T(8,128)(2,1)}, f32[8,256]{1,0:T(8,128)}) custom-call(s32[5]{0:T(128)} %stack.23.refs_0_.spot_ref, bf16[3,12288,256]{2,1,0:T(8,128)(2,1)} %build_dense.1.refs_1_, f32[16,1,768]{2,1,0:T(1,128)} %copy-done.10, bf16[256,768]{1,0:T(8,128)(2,1)} %bitcast.17, bf16[4096,768]{1,0:T(8,128)(2,1)} %all-gather.4.cloned.1.call-done.refs_4_), custom_call_target="tpu_custom_call" | custom-call | flops 4831838208 | bytes 25165824 | tf_op jit(solution)/shard_map/layer_first/layer/pallas_call | solution.py:176
  69.7 4.5 %collective-permute-start = (bf16[256,768]{1,0:T(8,128)(2,1)}, bf16[256,768]{1,0:T(8,128)(2,1)S(1)}, u32[]{:S(2)}, u32[]{:S(2)}) collective-permute-start(bf16[256,768]{1,0:T(8,128)(2,1)} %get-tuple-element.12.refs_4_), channel_id=1, source_target_pairs={{0,16},{1,17},{2,18},{3,19},{4,20},{5,21},{6,22},{7,23},{8,24},{9,... | collective-permute-start | bytes 1179656 | tf_op jit(solution)/shard_map/hand_over/ppermute | solution.py:432
  74.3 8.5 %collective-permute-done = bf16[256,768]{1,0:T(8,128)(2,1)S(1)} collective-permute-done((bf16[256,768]{1,0:T(8,128)(2,1)}, bf16[256,768]{1,0:T(8,128)(2,1)S(1)}, u32[]{:S(2)}, u32[]{:S(2)}) %collective-permute-start) | collective-permute-done | bytes 393248 | tf_op jit(solution)/shard_map/hand_over/ppermute | solution.py:432
  82.8 0.8 select_add_fusion
  83.6 1.3 collective-permute-start.2
  85.3 1.5 collective-permute-start.1
  86.8 1.9 %collective-permute-start.13 = (bf16[256,768]{1,0:T(8,128)(2,1)S(1)}, bf16[256,768]{1,0:T(8,128)(2,1)S(1)}, u32[]{:S(2)}, u32[]{:S(2)}) collective-permute-start(bf16[256,768]{1,0:T(8,128)(2,1)S(1)} %get-tuple-element.23.refs_1_.refs_3_.refs_5_), channel_id=1, source_target_pairs={{0,1},{1,0},{2,3},{3,2},{4,5},{5,4},{6,7},{7,6},{8,9},{9,8},{10,11... | collective-permute-start | bytes 1179656 | tf_op jit(solution)/shard_map/rows_second/ppermute | solution.py:377
  88.7 5.7 %collective-permute-done.2.refs_4_.refs_8_ = bf16[256,768]{1,0:T(8,128)(2,1)S(1)} collective-permute-done((bf16[256,768]{1,0:T(8,128)(2,1)S(1)}, bf16[256,768]{1,0:T(8,128)(2,1)S(1)}, u32[]{:S(2)}, u32[]{:S(2)}) %collective-permute-start.2) | collective-permute-done | bytes 393248 | tf_op jit(solution)/shard_map/rows_second/ppermute | solution.py:377
  94.9 2.7 %collective-permute-start.5 = (bf16[256,768]{1,0:T(8,128)(2,1)S(1)}, bf16[256,768]{1,0:T(8,128)(2,1)S(1)}, u32[]{:S(2)}, u32[]{:S(2)}) collective-permute-start(bf16[256,768]{1,0:T(8,128)(2,1)S(1)} %collective-permute-done.4.refs_5_.refs_9_), channel_id=1, source_target_pairs={{0,6},{1,7},{2,0},{3,1},{4,2},{5,3},{6,4},{7,5},{8,14},{9,15},{10,... | collective-permute-start | bytes 1179656 | tf_op jit(solution)/shard_map/rows_second/ppermute | solution.py:377
  97.6 2.8 %collective-permute-start.14 = (bf16[256,768]{1,0:T(8,128)(2,1)S(1)}, bf16[256,768]{1,0:T(8,128)(2,1)S(1)}, u32[]{:S(2)}, u32[]{:S(2)}) collective-permute-start(bf16[256,768]{1,0:T(8,128)(2,1)S(1)} %collective-permute-done.1.refs_2_.refs_6_), channel_id=1, source_target_pairs={{0,1},{1,0},{2,3},{3,2},{4,5},{5,4},{6,7},{7,6},{8,9},{9,8},{10,11... | collective-permute-start | bytes 1179656 | tf_op jit(solution)/shard_map/rows_second/ppermute | solution.py:377
  100.5 2.6 %collective-permute-done.6.refs_7_.refs_11_ = bf16[256,768]{1,0:T(8,128)(2,1)S(1)} collective-permute-done((bf16[256,768]{1,0:T(8,128)(2,1)S(1)}, bf16[256,768]{1,0:T(8,128)(2,1)S(1)}, u32[]{:S(2)}, u32[]{:S(2)}) %collective-permute-start.6) | collective-permute-done | bytes 393248 | tf_op jit(solution)/shard_map/rows_second/ppermute | solution.py:377
  103.1 2.8 %collective-permute-start.17 = (bf16[256,768]{1,0:T(8,128)(2,1)S(1)}, bf16[256,768]{1,0:T(8,128)(2,1)S(1)}, u32[]{:S(2)}, u32[]{:S(2)}) collective-permute-start(bf16[256,768]{1,0:T(8,128)(2,1)S(1)} %collective-permute-done.4.refs_5_.refs_9_), channel_id=1, source_target_pairs={{0,1},{1,0},{2,3},{3,2},{4,5},{5,4},{6,7},{7,6},{8,9},{9,8},{10,11... | collective-permute-start | bytes 1179656 | tf_op jit(solution)/shard_map/rows_second/ppermute | solution.py:377
  106.1 1.7 collective-permute-start.15
  108.3 3.0 %collective-permute-start.9 = (bf16[80,768]{1,0:T(8,128)(2,1)S(1)}, bf16[80,768]{1,0:T(8,128)(2,1)}, u32[]{:S(2)}, u32[]{:S(2)}) collective-permute-start(bf16[80,768]{1,0:T(8,128)(2,1)S(1)} %slice.14), channel_id=1, source_target_pairs={{0,6},{1,7},{2,0},{3,1},{4,2},{5,3},{6,4},{7,5},{8,14},{9,15},{10,... | collective-permute-start | bytes 368648 | tf_op jit(solution)/shard_map/rows_second/ppermute | solution.py:377
  111.4 0.9 collective-permute-start.7
  112.3 1.6 collective-permute-done.9.refs_10_.refs_14_
  113.9 1.1 collective-permute-start.21
  115.4 3.5 %collective-permute-start.20 = (bf16[96,768]{1,0:T(8,128)(2,1)S(1)}, bf16[96,768]{1,0:T(8,128)(2,1)}, u32[]{:S(2)}, u32[]{:S(2)}) collective-permute-start(bf16[96,768]{1,0:T(8,128)(2,1)S(1)} %collective-permute-done.7.refs_8_.refs_12_), channel_id=1, source_target_pairs={{0,1},{1,0},{2,3},{3,2},{4,5},{5,4},{6,7},{7,6},{8,9},{9,8},{10,11... | collective-permute-start | bytes 442376 | tf_op jit(solution)/shard_map/rows_second/ppermute | solution.py:377
  118.9 0.6 copy-done.19
  119.7 3.5 %pick.1 = (bf16[512,768]{1,0:T(8,128)(2,1)}, bf16[256,768]{1,0:T(8,128)(2,1)}, bf16[256,768]{1,0:T(8,128)(2,1)}, bf16[256,768]{1,0:T(8,128)(2,1)}) custom-call(s32[5]{0:T(128)} %stack.23.refs_0_.spot_ref, bf16[256,768]{1,0:T(8,128)(2,1)} %copy-done, bf16[256,768]{1,0:T(8,128)(2,1)} %copy-done.7, bf16[256,768]{1,0:T(8,128)(2,1)} %copy-done.2, ...), custom_call_target="tpu_custom_call" | custom-call | bytes 3932160 | tf_op jit(solution)/shard_map/hessian_rows/pick/pallas_call | solution.py:235
  123.2 1.3 collective-permute-start.10
  124.5 2.5 %collective-permute-start.11 = (bf16[256,768]{1,0:T(8,128)(2,1)}, bf16[256,768]{1,0:T(8,128)(2,1)S(1)}, u32[]{:S(2)}, u32[]{:S(2)}) collective-permute-start(bf16[256,768]{1,0:T(8,128)(2,1)} %get-tuple-element.15), channel_id=1, source_target_pairs={{0,64},{32,96},{64,0},{96,32},{1,65},{33,97},{65,1},{97,33},{2,66}... | collective-permute-start | bytes 1179656 | tf_op jit(solution)/shard_map/hessian_rows/ppermute | solution.py:362
  127.0 1.1 collective-permute-start.12
  128.1 14.4 %layer.3 = (bf16[256,768]{1,0:T(8,128)(2,1)}, f32[8,256]{1,0:T(8,128)}) custom-call(s32[5]{0:T(128)} %stack.23.refs_0_.spot_ref, bf16[3,12288,256]{2,1,0:T(8,128)(2,1)} %build_dense.1.refs_1_, f32[16,1,768]{2,1,0:T(1,128)} %copy-done.10, bf16[256,768]{1,0:T(8,128)(2,1)} %copy-done, bf16[256,768]{1,0:T(8,128)(2,1)} %get-tuple-element.12.refs_4_, ...), custom_call_target="tpu_custom_call" | custom-call | flops 4831838208 | bytes 25165824 | tf_op jit(solution)/shard_map/layer_second/layer/pallas_call | solution.py:176
  142.5 1.9 collective-permute-done.11.refs_1_
  144.4 0.7 copy-done.13
  145.3 0.9 collective-permute-start.28
  146.2 1.1 collective-permute-start.29
  147.3 2.8 %collective-permute-start.30 = (f32[8,256]{1,0:T(8,128)}, f32[8,256]{1,0:T(8,128)S(1)}, u32[]{:S(2)}, u32[]{:S(2)}) collective-permute-start(f32[8,256]{1,0:T(8,128)} %get-tuple-element.17.refs_3_.refs_14_), channel_id=1, source_target_pairs={{0,64},{32,96},{64,0},{96,32},{1,65},{33,97},{65,1},{97,33},{2,66}... | collective-permute-start | bytes 24584 | tf_op jit(solution)/shard_map/layer_second/ppermute | solution.py:362
  150.2 2.7 %collective-permute-start.23 = (bf16[512,768]{1,0:T(8,128)(2,1)S(1)}, bf16[512,768]{1,0:T(8,128)(2,1)S(1)}, u32[]{:S(2)}, u32[]{:S(2)}) collective-permute-start(bf16[512,768]{1,0:T(8,128)(2,1)S(1)} %copy-done.24), channel_id=1, source_target_pairs={{0,1},{1,0},{2,3},{3,2},{4,5},{5,4},{6,7},{7,6},{8,9},{9,8},{10,11... | collective-permute-start | bytes 2359304 | tf_op jit(solution)/shard_map/hessian/ppermute | solution.py:377
  153.0 0.8 collective-permute-start.32
  153.8 1.7 collective-permute-start.24
  155.4 1.6 collective-permute-start.25
  157.0 6.8 %collective-permute-done.27.refs_8_ = bf16[256,768]{1,0:T(8,128)(2,1)S(1)} collective-permute-done((bf16[256,768]{1,0:T(8,128)(2,1)}, bf16[256,768]{1,0:T(8,128)(2,1)S(1)}, u32[]{:S(2)}, u32[]{:S(2)}) %collective-permute-start.27) | collective-permute-done | bytes 393248 | tf_op jit(solution)/shard_map/hessian/ppermute | solution.py:387
  163.8 0.9 collective-permute-start.26
  164.7 1.3 collective-permute-start.34
  166.5 1.0 collective-permute-done.34.refs_12_
  167.6 0.9 collective-permute-done.33.refs_11_
  168.5 0.7 copy-done.31
  169.2 13.6 %gram.1 = f32[3072,768]{1,0:T(8,128)} custom-call(s32[5]{0:T(128)} %stack.23.refs_0_.spot_ref, bf16[512,768]{1,0:T(8,128)(2,1)} %get-tuple-element.13.refs_0_, bf16[256,768]{1,0:T(8,128)(2,1)} %get-tuple-element.18.refs_1_, bf16[256,768]{1,0:T(8,128)(2,1)} %get-tuple-element.19.refs_2_, bf16[256,768]{1,0:T(8,128)(2,1)} %get-tuple-element.20.refs_3_, ...), custom_call_target="tpu_custom_call" | custom-call | flops 4831838208 | bytes 17301504 | tf_op jit(solution)/shard_map/hessian/gram/pallas_call | solution.py:336
  (112 shorter events, 3.9 us)
Async XLA Ops:
  7.2 23.3 %copy-start.23 = (s32[1,12,48]{2,0,1:T(1,128)S(1)}, s32[1,12,48]{2,0,1:T(1,128)}, u32[]{:S(2)}) copy-start(s32[1,12,48]{2,0,1:T(1,128)} %param.7) | copy-start | bytes 6916
  7.2 48.6 %all-gather.4.cloned.1.call-start = ((), (), s32[]{:S(2)}) async-start(), calls=%async_computation.1 | async-start | bytes 6684672 | tf_op jit(solution)/shard_map/rows_first/all_gather | solution.py:421
  9.3 36.2 %all-to-all-start = ((f32[16,1,768]{2,1,0:T(1,128)}), f32[16,1,768]{2,1,0:T(1,128)S(1)}, u32[]{:S(2)}, u32[]{:S(2)}) async-start(f32[16,1,768]{2,1,0:T(1,128)} %broadcast_in_dim.13), calls=%async_computation | async-start | bytes 98304 | tf_op jit(solution)/shard_map/gains/all_to_all | solution.py:423
  16.6 103.0 %all-gather.6.cloned.1.call-start = ((), (), s32[]{:S(2)}) async-start(), calls=%async_computation.2 | async-start | bytes 1966080 | tf_op jit(solution)/shard_map/columns/all_gather | solution.py:435
  45.5 37.3 %copy-start.1 = (bf16[4,64,768]{2,1,0:T(8,128)(2,1)S(1)}, bf16[4,64,768]{2,1,0:T(8,128)(2,1)}, u32[]{:S(2)}) copy-start(bf16[4,64,768]{2,1,0:T(8,128)(2,1)} %param.4) | copy-start | bytes 1179652
  69.7 13.1 %collective-permute-start = (bf16[256,768]{1,0:T(8,128)(2,1)}, bf16[256,768]{1,0:T(8,128)(2,1)S(1)}, u32[]{:S(2)}, u32[]{:S(2)}) collective-permute-start(bf16[256,768]{1,0:T(8,128)(2,1)} %get-tuple-element.12.refs_4_), channel_id=1, source_target_pairs={{0,16},{1,17},{2,18},{3,19},{4,20},{5,21},{6,22},{7,23},{8,24},{9,... | collective-permute-start | bytes 1179656 | tf_op jit(solution)/shard_map/hand_over/ppermute | solution.py:432
  83.6 36.0 %copy-start = (bf16[256,768]{1,0:T(8,128)(2,1)}, bf16[256,768]{1,0:T(8,128)(2,1)S(1)}, u32[]{:S(2)}) copy-start(bf16[256,768]{1,0:T(8,128)(2,1)S(1)} %get-tuple-element.23.refs_1_.refs_3_.refs_5_) | copy-start | bytes 1179652
  83.6 10.8 %collective-permute-start.2 = (bf16[256,768]{1,0:T(8,128)(2,1)S(1)}, bf16[256,768]{1,0:T(8,128)(2,1)S(1)}, u32[]{:S(2)}, u32[]{:S(2)}) collective-permute-start(bf16[256,768]{1,0:T(8,128)(2,1)S(1)} %get-tuple-element.23.refs_1_.refs_3_.refs_5_), channel_id=1, source_target_pairs={{0,2},{1,3},{2,4},{3,5},{4,6},{5,7},{6,0},{7,1},{8,10},{9,11},{10,... | collective-permute-start | bytes 1179656 | tf_op jit(solution)/shard_map/rows_second/ppermute | solution.py:377
  84.9 10.0 %collective-permute-start.4 = (bf16[256,768]{1,0:T(8,128)(2,1)S(1)}, bf16[256,768]{1,0:T(8,128)(2,1)S(1)}, u32[]{:S(2)}, u32[]{:S(2)}) collective-permute-start(bf16[256,768]{1,0:T(8,128)(2,1)S(1)} %get-tuple-element.23.refs_1_.refs_3_.refs_5_), channel_id=1, source_target_pairs={{0,8},{1,9},{2,10},{3,11},{4,12},{5,13},{6,14},{7,15},{8,0},{9,1},... | collective-permute-start | bytes 1179656 | tf_op jit(solution)/shard_map/rows_second/ppermute | solution.py:377
  85.3 12.2 %collective-permute-start.1 = (bf16[256,768]{1,0:T(8,128)(2,1)S(1)}, bf16[256,768]{1,0:T(8,128)(2,1)S(1)}, u32[]{:S(2)}, u32[]{:S(2)}) collective-permute-start(bf16[256,768]{1,0:T(8,128)(2,1)S(1)} %get-tuple-element.23.refs_1_.refs_3_.refs_5_), channel_id=1, source_target_pairs={{0,6},{1,7},{2,0},{3,1},{4,2},{5,3},{6,4},{7,5},{8,14},{9,15},{10,... | collective-permute-start | bytes 1179656 | tf_op jit(solution)/shard_map/rows_second/ppermute | solution.py:377
  86.8 13.6 %collective-permute-start.13 = (bf16[256,768]{1,0:T(8,128)(2,1)S(1)}, bf16[256,768]{1,0:T(8,128)(2,1)S(1)}, u32[]{:S(2)}, u32[]{:S(2)}) collective-permute-start(bf16[256,768]{1,0:T(8,128)(2,1)S(1)} %get-tuple-element.23.refs_1_.refs_3_.refs_5_), channel_id=1, source_target_pairs={{0,1},{1,0},{2,3},{3,2},{4,5},{5,4},{6,7},{7,6},{8,9},{9,8},{10,11... | collective-permute-start | bytes 1179656 | tf_op jit(solution)/shard_map/rows_second/ppermute | solution.py:377
  94.4 25.2 %copy-start.5 = (bf16[256,768]{1,0:T(8,128)(2,1)}, bf16[256,768]{1,0:T(8,128)(2,1)S(1)}, u32[]{:S(2)}) copy-start(bf16[256,768]{1,0:T(8,128)(2,1)S(1)} %collective-permute-done.2.refs_4_.refs_8_) | copy-start | bytes 1179652
  94.4 8.7 %collective-permute-start.6 = (bf16[256,768]{1,0:T(8,128)(2,1)S(1)}, bf16[256,768]{1,0:T(8,128)(2,1)S(1)}, u32[]{:S(2)}, u32[]{:S(2)}) collective-permute-start(bf16[256,768]{1,0:T(8,128)(2,1)S(1)} %collective-permute-done.2.refs_4_.refs_8_), channel_id=1, source_target_pairs={{0,8},{1,9},{2,10},{3,11},{4,12},{5,13},{6,14},{7,15},{8,0},{9,1},... | collective-permute-start | bytes 1179656 | tf_op jit(solution)/shard_map/rows_second/ppermute | solution.py:377
  94.9 11.1 %collective-permute-start.3 = (bf16[256,768]{1,0:T(8,128)(2,1)S(1)}, bf16[256,768]{1,0:T(8,128)(2,1)S(1)}, u32[]{:S(2)}, u32[]{:S(2)}) collective-permute-start(bf16[256,768]{1,0:T(8,128)(2,1)S(1)} %collective-permute-done.2.refs_4_.refs_8_), channel_id=1, source_target_pairs={{0,2},{1,3},{2,4},{3,5},{4,6},{5,7},{6,0},{7,1},{8,10},{9,11},{10,... | collective-permute-start | bytes 1179656 | tf_op jit(solution)/shard_map/rows_second/ppermute | solution.py:377
  94.9 24.7 %copy-start.6 = (bf16[256,768]{1,0:T(8,128)(2,1)}, bf16[256,768]{1,0:T(8,128)(2,1)S(1)}, u32[]{:S(2)}) copy-start(bf16[256,768]{1,0:T(8,128)(2,1)S(1)} %collective-permute-done.4.refs_5_.refs_9_) | copy-start | bytes 1179652
  94.9 11.2 %collective-permute-start.5 = (bf16[256,768]{1,0:T(8,128)(2,1)S(1)}, bf16[256,768]{1,0:T(8,128)(2,1)S(1)}, u32[]{:S(2)}, u32[]{:S(2)}) collective-permute-start(bf16[256,768]{1,0:T(8,128)(2,1)S(1)} %collective-permute-done.4.refs_5_.refs_9_), channel_id=1, source_target_pairs={{0,6},{1,7},{2,0},{3,1},{4,2},{5,3},{6,4},{7,5},{8,14},{9,15},{10,... | collective-permute-start | bytes 1179656 | tf_op jit(solution)/shard_map/rows_second/ppermute | solution.py:377
  97.6 22.0 %copy-start.7 = (bf16[256,768]{1,0:T(8,128)(2,1)}, bf16[256,768]{1,0:T(8,128)(2,1)S(1)}, u32[]{:S(2)}) copy-start(bf16[256,768]{1,0:T(8,128)(2,1)S(1)} %collective-permute-done.1.refs_2_.refs_6_) | copy-start | bytes 1179652
  97.6 10.2 %collective-permute-start.14 = (bf16[256,768]{1,0:T(8,128)(2,1)S(1)}, bf16[256,768]{1,0:T(8,128)(2,1)S(1)}, u32[]{:S(2)}, u32[]{:S(2)}) collective-permute-start(bf16[256,768]{1,0:T(8,128)(2,1)S(1)} %collective-permute-done.1.refs_2_.refs_6_), channel_id=1, source_target_pairs={{0,1},{1,0},{2,3},{3,2},{4,5},{5,4},{6,7},{7,6},{8,9},{9,8},{10,11... | collective-permute-start | bytes 1179656 | tf_op jit(solution)/shard_map/rows_second/ppermute | solution.py:377
  100.4 7.4 %collective-permute-start.16 = (bf16[256,768]{1,0:T(8,128)(2,1)S(1)}, bf16[256,768]{1,0:T(8,128)(2,1)S(1)}, u32[]{:S(2)}, u32[]{:S(2)}) collective-permute-start(bf16[256,768]{1,0:T(8,128)(2,1)S(1)} %collective-permute-done.2.refs_4_.refs_8_), channel_id=1, source_target_pairs={{0,1},{1,0},{2,3},{3,2},{4,5},{5,4},{6,7},{7,6},{8,9},{9,8},{10,11... | collective-permute-start | bytes 1179656 | tf_op jit(solution)/shard_map/rows_second/ppermute | solution.py:377
  103.1 16.5 %copy-start.3 = (bf16[256,768]{1,0:T(8,128)(2,1)}, bf16[256,768]{1,0:T(8,128)(2,1)S(1)}, u32[]{:S(2)}) copy-start(bf16[256,768]{1,0:T(8,128)(2,1)S(1)} %collective-permute-done.6.refs_7_.refs_11_) | copy-start | bytes 1179652
  103.1 5.2 %collective-permute-start.17 = (bf16[256,768]{1,0:T(8,128)(2,1)S(1)}, bf16[256,768]{1,0:T(8,128)(2,1)S(1)}, u32[]{:S(2)}, u32[]{:S(2)}) collective-permute-start(bf16[256,768]{1,0:T(8,128)(2,1)S(1)} %collective-permute-done.4.refs_5_.refs_9_), channel_id=1, source_target_pairs={{0,1},{1,0},{2,3},{3,2},{4,5},{5,4},{6,7},{7,6},{8,9},{9,8},{10,11... | collective-permute-start | bytes 1179656 | tf_op jit(solution)/shard_map/rows_second/ppermute | solution.py:377
  106.0 13.7 %copy-start.2 = (bf16[256,768]{1,0:T(8,128)(2,1)}, bf16[256,768]{1,0:T(8,128)(2,1)S(1)}, u32[]{:S(2)}) copy-start(bf16[256,768]{1,0:T(8,128)(2,1)S(1)} %collective-permute-done.3.refs_3_.refs_7_) | copy-start | bytes 1179652
  106.0 5.4 %collective-permute-start.8 = (bf16[80,768]{1,0:T(8,128)(2,1)S(1)}, bf16[80,768]{1,0:T(8,128)(2,1)S(1)}, u32[]{:S(2)}, u32[]{:S(2)}) collective-permute-start(bf16[80,768]{1,0:T(8,128)(2,1)S(1)} %slice.13), channel_id=1, source_target_pairs={{0,2},{1,3},{2,4},{3,5},{4,6},{5,7},{6,0},{7,1},{8,10},{9,11},{10,... | collective-permute-start | bytes 368648 | tf_op jit(solution)/shard_map/rows_second/ppermute | solution.py:377
  106.1 20.9 %collective-permute-start.15 = (bf16[256,768]{1,0:T(8,128)(2,1)S(1)}, bf16[256,768]{1,0:T(8,128)(2,1)}, u32[]{:S(2)}, u32[]{:S(2)}) collective-permute-start(bf16[256,768]{1,0:T(8,128)(2,1)S(1)} %collective-permute-done.3.refs_3_.refs_7_), channel_id=1, source_target_pairs={{0,1},{1,0},{2,3},{3,2},{4,5},{5,4},{6,7},{7,6},{8,9},{9,8},{10,11... | collective-permute-start | bytes 1179656 | tf_op jit(solution)/shard_map/rows_second/ppermute | solution.py:377
  107.7 20.3 %collective-permute-start.18 = (bf16[256,768]{1,0:T(8,128)(2,1)S(1)}, bf16[256,768]{1,0:T(8,128)(2,1)}, u32[]{:S(2)}, u32[]{:S(2)}) collective-permute-start(bf16[256,768]{1,0:T(8,128)(2,1)S(1)} %collective-permute-done.5.refs_6_.refs_10_), channel_id=1, source_target_pairs={{0,1},{1,0},{2,3},{3,2},{4,5},{5,4},{6,7},{7,6},{8,9},{9,8},{10,11... | collective-permute-start | bytes 1179656 | tf_op jit(solution)/shard_map/rows_second/ppermute | solution.py:377
  107.9 20.2 %collective-permute-start.19 = (bf16[256,768]{1,0:T(8,128)(2,1)S(1)}, bf16[256,768]{1,0:T(8,128)(2,1)}, u32[]{:S(2)}, u32[]{:S(2)}) collective-permute-start(bf16[256,768]{1,0:T(8,128)(2,1)S(1)} %collective-permute-done.6.refs_7_.refs_11_), channel_id=1, source_target_pairs={{0,1},{1,0},{2,3},{3,2},{4,5},{5,4},{6,7},{7,6},{8,9},{9,8},{10,11... | collective-permute-start | bytes 1179656 | tf_op jit(solution)/shard_map/rows_second/ppermute | solution.py:377
  108.3 5.6 %collective-permute-start.9 = (bf16[80,768]{1,0:T(8,128)(2,1)S(1)}, bf16[80,768]{1,0:T(8,128)(2,1)}, u32[]{:S(2)}, u32[]{:S(2)}) collective-permute-start(bf16[80,768]{1,0:T(8,128)(2,1)S(1)} %slice.14), channel_id=1, source_target_pairs={{0,6},{1,7},{2,0},{3,1},{4,2},{5,3},{6,4},{7,5},{8,14},{9,15},{10,... | collective-permute-start | bytes 368648 | tf_op jit(solution)/shard_map/rows_second/ppermute | solution.py:377
  111.4 4.0 %collective-permute-start.7 = (bf16[96,768]{1,0:T(8,128)(2,1)S(1)}, bf16[96,768]{1,0:T(8,128)(2,1)S(1)}, u32[]{:S(2)}, u32[]{:S(2)}) collective-permute-start(bf16[96,768]{1,0:T(8,128)(2,1)S(1)} %slice.12), channel_id=1, source_target_pairs={{0,8},{1,9},{2,10},{3,11},{4,12},{5,13},{6,14},{7,15},{8,0},{9,1},... | collective-permute-start | bytes 442376 | tf_op jit(solution)/shard_map/rows_second/ppermute | solution.py:377
  113.9 5.0 %collective-permute-start.21 = (bf16[80,768]{1,0:T(8,128)(2,1)S(1)}, bf16[80,768]{1,0:T(8,128)(2,1)S(1)}, u32[]{:S(2)}, u32[]{:S(2)}) collective-permute-start(bf16[80,768]{1,0:T(8,128)(2,1)S(1)} %collective-permute-done.8.refs_9_.refs_13_), channel_id=1, source_target_pairs={{0,1},{1,0},{2,3},{3,2},{4,5},{5,4},{6,7},{7,6},{8,9},{9,8},{10,11... | collective-permute-start | bytes 368648 | tf_op jit(solution)/shard_map/rows_second/ppermute | solution.py:377
  115.4 9.1 %collective-permute-start.20 = (bf16[96,768]{1,0:T(8,128)(2,1)S(1)}, bf16[96,768]{1,0:T(8,128)(2,1)}, u32[]{:S(2)}, u32[]{:S(2)}) collective-permute-start(bf16[96,768]{1,0:T(8,128)(2,1)S(1)} %collective-permute-done.7.refs_8_.refs_12_), channel_id=1, source_target_pairs={{0,1},{1,0},{2,3},{3,2},{4,5},{5,4},{6,7},{7,6},{8,9},{9,8},{10,11... | collective-permute-start | bytes 442376 | tf_op jit(solution)/shard_map/rows_second/ppermute | solution.py:377
  119.6 3.7 %collective-permute-start.22 = (bf16[80,768]{1,0:T(8,128)(2,1)}, bf16[80,768]{1,0:T(8,128)(2,1)}, u32[]{:S(2)}, u32[]{:S(2)}) collective-permute-start(bf16[80,768]{1,0:T(8,128)(2,1)} %collective-permute-done.9.refs_10_.refs_14_), channel_id=1, source_target_pairs={{0,1},{1,0},{2,3},{3,2},{4,5},{5,4},{6,7},{7,6},{8,9},{9,8},{10,11... | collective-permute-start | bytes 368648 | tf_op jit(solution)/shard_map/rows_second/ppermute | solution.py:377
  123.2 19.2 %collective-permute-start.10 = (bf16[256,768]{1,0:T(8,128)(2,1)}, bf16[256,768]{1,0:T(8,128)(2,1)S(1)}, u32[]{:S(2)}, u32[]{:S(2)}) collective-permute-start(bf16[256,768]{1,0:T(8,128)(2,1)} %get-tuple-element.14), channel_id=1, source_target_pairs={{0,32},{32,64},{64,96},{96,0},{1,33},{33,65},{65,97},{97,1},{2,34}... | collective-permute-start | bytes 1179656 | tf_op jit(solution)/shard_map/hessian_rows/ppermute | solution.py:362
  124.5 19.9 %collective-permute-start.11 = (bf16[256,768]{1,0:T(8,128)(2,1)}, bf16[256,768]{1,0:T(8,128)(2,1)S(1)}, u32[]{:S(2)}, u32[]{:S(2)}) collective-permute-start(bf16[256,768]{1,0:T(8,128)(2,1)} %get-tuple-element.15), channel_id=1, source_target_pairs={{0,64},{32,96},{64,0},{96,32},{1,65},{33,97},{65,1},{97,33},{2,66}... | collective-permute-start | bytes 1179656 | tf_op jit(solution)/shard_map/hessian_rows/ppermute | solution.py:362
  127.0 23.2 %copy-start.24 = (bf16[512,768]{1,0:T(8,128)(2,1)S(1)}, bf16[512,768]{1,0:T(8,128)(2,1)}, u32[]{:S(2)}) copy-start(bf16[512,768]{1,0:T(8,128)(2,1)} %get-tuple-element.13.refs_0_) | copy-start | bytes 2359300
  127.0 17.4 %collective-permute-start.12 = (bf16[256,768]{1,0:T(8,128)(2,1)}, bf16[256,768]{1,0:T(8,128)(2,1)S(1)}, u32[]{:S(2)}, u32[]{:S(2)}) collective-permute-start(bf16[256,768]{1,0:T(8,128)(2,1)} %get-tuple-element.16), channel_id=1, source_target_pairs={{0,96},{32,0},{64,32},{96,64},{1,97},{33,1},{65,33},{97,65},{2,98}... | collective-permute-start | bytes 1179656 | tf_op jit(solution)/shard_map/hessian_rows/ppermute | solution.py:362
  145.3 10.2 %collective-permute-start.28 = (bf16[256,768]{1,0:T(8,128)(2,1)}, bf16[256,768]{1,0:T(8,128)(2,1)S(1)}, u32[]{:S(2)}, u32[]{:S(2)}) collective-permute-start(bf16[256,768]{1,0:T(8,128)(2,1)} %get-tuple-element.19.refs_2_), channel_id=1, source_target_pairs={{0,8},{1,9},{2,10},{3,11},{4,12},{5,13},{6,14},{7,15},{8,0},{9,1},... | collective-permute-start | bytes 1179656 | tf_op jit(solution)/shard_map/hessian/ppermute | solution.py:387
  146.2 6.8 %collective-permute-start.29 = (f32[8,256]{1,0:T(8,128)}, f32[8,256]{1,0:T(8,128)S(1)}, u32[]{:S(2)}, u32[]{:S(2)}) collective-permute-start(f32[8,256]{1,0:T(8,128)} %get-tuple-element.17.refs_3_.refs_14_), channel_id=1, source_target_pairs={{0,32},{32,64},{64,96},{96,0},{1,33},{33,65},{65,97},{97,1},{2,34}... | collective-permute-start | bytes 24584 | tf_op jit(solution)/shard_map/layer_second/ppermute | solution.py:362
  147.3 5.6 %collective-permute-start.30 = (f32[8,256]{1,0:T(8,128)}, f32[8,256]{1,0:T(8,128)S(1)}, u32[]{:S(2)}, u32[]{:S(2)}) collective-permute-start(f32[8,256]{1,0:T(8,128)} %get-tuple-element.17.refs_3_.refs_14_), channel_id=1, source_target_pairs={{0,64},{32,96},{64,0},{96,32},{1,65},{33,97},{65,1},{97,33},{2,66}... | collective-permute-start | bytes 24584 | tf_op jit(solution)/shard_map/layer_second/ppermute | solution.py:362
  150.1 3.7 %collective-permute-start.31 = (f32[8,256]{1,0:T(8,128)}, f32[8,256]{1,0:T(8,128)S(1)}, u32[]{:S(2)}, u32[]{:S(2)}) collective-permute-start(f32[8,256]{1,0:T(8,128)} %get-tuple-element.17.refs_3_.refs_14_), channel_id=1, source_target_pairs={{0,96},{32,0},{64,32},{96,64},{1,97},{33,1},{65,33},{97,65},{2,98}... | collective-permute-start | bytes 24584 | tf_op jit(solution)/shard_map/layer_second/ppermute | solution.py:362
  150.2 16.3 %collective-permute-start.23 = (bf16[512,768]{1,0:T(8,128)(2,1)S(1)}, bf16[512,768]{1,0:T(8,128)(2,1)S(1)}, u32[]{:S(2)}, u32[]{:S(2)}) collective-permute-start(bf16[512,768]{1,0:T(8,128)(2,1)S(1)} %copy-done.24), channel_id=1, source_target_pairs={{0,1},{1,0},{2,3},{3,2},{4,5},{5,4},{6,7},{7,6},{8,9},{9,8},{10,11... | collective-permute-start | bytes 2359304 | tf_op jit(solution)/shard_map/hessian/ppermute | solution.py:377
  152.9 10.9 %collective-permute-start.27 = (bf16[256,768]{1,0:T(8,128)(2,1)}, bf16[256,768]{1,0:T(8,128)(2,1)S(1)}, u32[]{:S(2)}, u32[]{:S(2)}) collective-permute-start(bf16[256,768]{1,0:T(8,128)(2,1)} %get-tuple-element.18.refs_1_), channel_id=1, source_target_pairs={{0,2},{1,3},{2,0},{3,1},{4,6},{5,7},{6,4},{7,5},{8,10},{9,11},{10,... | collective-permute-start | bytes 1179656 | tf_op jit(solution)/shard_map/hessian/ppermute | solution.py:387
  153.0 11.7 %collective-permute-start.32 = (bf16[256,768]{1,0:T(8,128)(2,1)}, bf16[256,768]{1,0:T(8,128)(2,1)S(1)}, u32[]{:S(2)}, u32[]{:S(2)}) collective-permute-start(bf16[256,768]{1,0:T(8,128)(2,1)} %get-tuple-element.20.refs_3_), channel_id=1, source_target_pairs={{0,6},{1,7},{2,4},{3,5},{4,2},{5,3},{6,0},{7,1},{8,14},{9,15},{10,... | collective-permute-start | bytes 1179656 | tf_op jit(solution)/shard_map/hessian/ppermute | solution.py:387
  153.8 12.2 %collective-permute-start.24 = (bf16[256,768]{1,0:T(8,128)(2,1)}, bf16[256,768]{1,0:T(8,128)(2,1)S(1)}, u32[]{:S(2)}, u32[]{:S(2)}) collective-permute-start(bf16[256,768]{1,0:T(8,128)(2,1)} %get-tuple-element.18.refs_1_), channel_id=1, source_target_pairs={{0,1},{1,0},{2,3},{3,2},{4,5},{5,4},{6,7},{7,6},{8,9},{9,8},{10,11... | collective-permute-start | bytes 1179656 | tf_op jit(solution)/shard_map/hessian/ppermute | solution.py:377
  155.4 10.7 %collective-permute-start.25 = (bf16[256,768]{1,0:T(8,128)(2,1)}, bf16[256,768]{1,0:T(8,128)(2,1)}, u32[]{:S(2)}, u32[]{:S(2)}) collective-permute-start(bf16[256,768]{1,0:T(8,128)(2,1)} %get-tuple-element.19.refs_2_), channel_id=1, source_target_pairs={{0,1},{1,0},{2,3},{3,2},{4,5},{5,4},{6,7},{7,6},{8,9},{9,8},{10,11... | collective-permute-start | bytes 1179656 | tf_op jit(solution)/shard_map/hessian/ppermute | solution.py:377
  163.8 2.7 %collective-permute-start.26 = (bf16[256,768]{1,0:T(8,128)(2,1)}, bf16[256,768]{1,0:T(8,128)(2,1)S(1)}, u32[]{:S(2)}, u32[]{:S(2)}) collective-permute-start(bf16[256,768]{1,0:T(8,128)(2,1)} %get-tuple-element.20.refs_3_), channel_id=1, source_target_pairs={{0,1},{1,0},{2,3},{3,2},{4,5},{5,4},{6,7},{7,6},{8,9},{9,8},{10,11... | collective-permute-start | bytes 1179656 | tf_op jit(solution)/shard_map/hessian/ppermute | solution.py:377
  164.7 2.9 %collective-permute-start.34 = (bf16[256,768]{1,0:T(8,128)(2,1)}, bf16[256,768]{1,0:T(8,128)(2,1)S(1)}, u32[]{:S(2)}, u32[]{:S(2)}) collective-permute-start(bf16[256,768]{1,0:T(8,128)(2,1)} %after.3.refs_9_), channel_id=1, source_target_pairs={{0,1},{1,0},{2,3},{3,2},{4,5},{5,4},{6,7},{7,6},{8,9},{9,8},{10,11... | collective-permute-start | bytes 1179656 | tf_op jit(solution)/shard_map/hessian/ppermute | solution.py:377
  166.0 2.5 %collective-permute-start.33 = (bf16[256,768]{1,0:T(8,128)(2,1)S(1)}, bf16[256,768]{1,0:T(8,128)(2,1)S(1)}, u32[]{:S(2)}, u32[]{:S(2)}) collective-permute-start(bf16[256,768]{1,0:T(8,128)(2,1)S(1)} %collective-permute-done.27.refs_8_), channel_id=1, source_target_pairs={{0,1},{1,0},{2,3},{3,2},{4,5},{5,4},{6,7},{7,6},{8,9},{9,8},{10,11... | collective-permute-start | bytes 1179656 | tf_op jit(solution)/shard_map/hessian/ppermute | solution.py:377
  166.1 3.1 %collective-permute-start.35 = (bf16[256,768]{1,0:T(8,128)(2,1)S(1)}, bf16[256,768]{1,0:T(8,128)(2,1)}, u32[]{:S(2)}, u32[]{:S(2)}) collective-permute-start(bf16[256,768]{1,0:T(8,128)(2,1)S(1)} %collective-permute-done.32.refs_10_), channel_id=1, source_target_pairs={{0,1},{1,0},{2,3},{3,2},{4,5},{5,4},{6,7},{7,6},{8,9},{9,8},{10,11... | collective-permute-start | bytes 1179656 | tf_op jit(solution)/shard_map/hessian/ppermute | solution.py:377
  (23 other events, 108.5 us)
Sparse Core Ops, SparseCore 0:
  9.7 46.0 all-gather.3
  83.7 28.5 all-gather.5

commit v2 on v1

--- a/solution.py
+++ b/solution.py
@@ -97,6 +97,8 @@
         return pltpu.make_async_copy(weight_ref.at[:, span], weight.at[:, into], weight_sems.at[position])
 
     start_pieces(pieces, sources, rows, sems)
+    weight_copy(0).start()
+    weight_copy(1).start()
     means[...] = jnp.zeros_like(means)
     scales[...] = jnp.zeros_like(scales)
     total[...] = own_ref[...].astype(jnp.float32)
@@ -114,7 +116,10 @@
                     squared = squared + values * values
                 means[span] += added
                 scales[span] += squared
-        weight_copy(pair).start()
+
+        @pl.when(pair + 2 < TENSOR // 2)
+        def _():
+            weight_copy(pair + 2).start()
 
     mean = jnp.sum(means[...], axis=1, keepdims=True) / D
     square = jnp.sum(scales[...], axis=1, keepdims=True) / D

time: 191 us -> 190 us (level)
  no operation moved by 1% of the time
where the time goes in v2:
time: 190 us
  Pallas kernels  59 us (31%)
  starting transfers between devices  56 us (29%)
  waiting for transfers between devices  40.7 us (21%)
  local copies, waits for them, and re-layouts  18.1 us (10%)
  between operations  14.4 us (8%)
    ppermute x26, starting transfers between devices, shift(): return lax.ppermute(value, 'tensor', pairs)  33.4 us
    pallas_call x2, Pallas kernels, layer(): pl.pallas_call(lambda *refs: layer_kernel(pieces, count, straight, *refs)...  28 us
    pallas_call x1, Pallas kernels, build_dense(): pl.pallas_call(build_kernel, grid_spec=pltpu.PrefetchScalarGridSpec(num_s...  13.8 us
    squeeze x1, local copies, waits for them, and re-layouts, build_dense(): blocks = values.reshape(WIDTH // BLOCK, KEEP, BLOCK, BLOCK)  13.8 us
    pallas_call x1, Pallas kernels, gram(): pl.pallas_call(gram_kernel, in_specs=[SMEM] + [ANY] * (4 * DP - 2) + [VME...  13.6 us
    ppermute x26, waiting for transfers between devices, shift(): return lax.ppermute(value, 'tensor', pairs)  12.3 us
    all_gather x1, waiting for transfers between devices, body(): gathered = lax.all_gather(own, 'tensor', axis=0, tiled=True)  10.3 us
    ppermute x6, starting transfers between devices, along_dp(): lax.ppermute(value, 'dp', [(source, (source + step) % DP) for source in r...  8.92 us
  transfers between devices with their start and end apart: 39, of which 11 were waited for; matrix products, arithmetic and copies ran while one was open for 9% of the time, Pallas kernels for 17%

profile of v2, /device:TPU:1, one launch (start us, length us, event | category | flops | bytes accessed | tf_op | source)
XLA Modules:
  0.0 189.7 jit_solution(11050885994881190450)
XLA Ops:
  7.2 0.7 all-gather.4.cloned.1.call-update
  7.9 0.7 reduce
  8.6 0.6 broadcast_in_dim.13
  9.3 7.3 %all-to-all-start = ((f32[16,1,768]{2,1,0:T(1,128)}), f32[16,1,768]{2,1,0:T(1,128)S(1)}, u32[]{:S(2)}, u32[]{:S(2)}) async-start(f32[16,1,768]{2,1,0:T(1,128)} %broadcast_in_dim.13), calls=%async_computation | async-start | bytes 98304 | tf_op jit(solution)/shard_map/gains/all_to_all | solution.py:428
  16.7 13.8 %squeeze.7.blocks_ref = bf16[12,48,64,64]{3,2,1,0:T(8,128)(2,1)} reshape(bf16[1,12,48,4096]{3,2,1,0:T(8,128)(2,1)} %param.6) | data formatting | bytes 9437184 | tf_op jit(solution)/shard_map/weight/reshape;weight/squeeze | solution.py:47
  31.1 13.8 %build_dense.1.refs_1_ = bf16[3,12288,256]{2,1,0:T(8,128)(2,1)} custom-call(s32[12,48]{1,0:T(8,128)} %bitcast.20, bf16[12,48,64,64]{3,2,1,0:T(8,128)(2,1)} %squeeze.7.blocks_ref), custom_call_target="tpu_custom_call" | custom-call | bytes 33554432 | tf_op jit(solution)/shard_map/weight/build_dense/pallas_call | solution.py:49
  44.9 0.6 stack.23.refs_0_.spot_ref
  45.5 10.3 %all-gather.4.cloned.1.call-done.refs_4_ = bf16[4096,768]{1,0:T(8,128)(2,1)} async-done(((bf16[256,768]{1,0:T(8,128)(2,1)}), bf16[4096,768]{1,0:T(8,128)(2,1)}) %all-gather.4.cloned.1.call-update) | async-done | bytes 6291472 | tf_op jit(solution)/shard_map/rows_first/all_gather | solution.py:426
  55.8 13.9 %layer.2 = (bf16[256,768]{1,0:T(8,128)(2,1)}, f32[8,256]{1,0:T(8,128)}) custom-call(s32[5]{0:T(128)} %stack.23.refs_0_.spot_ref, bf16[3,12288,256]{2,1,0:T(8,128)(2,1)} %build_dense.1.refs_1_, f32[16,1,768]{2,1,0:T(1,128)} %copy-done.10, bf16[256,768]{1,0:T(8,128)(2,1)} %bitcast.17, bf16[4096,768]{1,0:T(8,128)(2,1)} %all-gather.4.cloned.1.call-done.refs_4_), custom_call_target="tpu_custom_call" | custom-call | flops 4831838208 | bytes 25165824 | tf_op jit(solution)/shard_map/layer_first/layer/pallas_call | solution.py:181
  69.7 4.5 %collective-permute-start = (bf16[256,768]{1,0:T(8,128)(2,1)}, bf16[256,768]{1,0:T(8,128)(2,1)S(1)}, u32[]{:S(2)}, u32[]{:S(2)}) collective-permute-start(bf16[256,768]{1,0:T(8,128)(2,1)} %get-tuple-element.12.refs_4_), channel_id=1, source_target_pairs={{0,16},{1,17},{2,18},{3,19},{4,20},{5,21},{6,22},{7,23},{8,24},{9,... | collective-permute-start | bytes 1179656 | tf_op jit(solution)/shard_map/hand_over/ppermute | solution.py:437
  74.2 8.5 %collective-permute-done = bf16[256,768]{1,0:T(8,128)(2,1)S(1)} collective-permute-done((bf16[256,768]{1,0:T(8,128)(2,1)}, bf16[256,768]{1,0:T(8,128)(2,1)S(1)}, u32[]{:S(2)}, u32[]{:S(2)}) %collective-permute-start) | collective-permute-done | bytes 393248 | tf_op jit(solution)/shard_map/hand_over/ppermute | solution.py:437
  82.7 0.8 select_add_fusion
  83.6 1.3 collective-permute-start.2
  85.3 1.5 collective-permute-start.1
  86.8 1.9 %collective-permute-start.13 = (bf16[256,768]{1,0:T(8,128)(2,1)S(1)}, bf16[256,768]{1,0:T(8,128)(2,1)S(1)}, u32[]{:S(2)}, u32[]{:S(2)}) collective-permute-start(bf16[256,768]{1,0:T(8,128)(2,1)S(1)} %get-tuple-element.23.refs_1_.refs_3_.refs_5_), channel_id=1, source_target_pairs={{0,1},{1,0},{2,3},{3,2},{4,5},{5,4},{6,7},{7,6},{8,9},{9,8},{10,11... | collective-permute-start | bytes 1179656 | tf_op jit(solution)/shard_map/rows_second/ppermute | solution.py:382
  88.7 5.7 %collective-permute-done.2.refs_4_.refs_8_ = bf16[256,768]{1,0:T(8,128)(2,1)S(1)} collective-permute-done((bf16[256,768]{1,0:T(8,128)(2,1)S(1)}, bf16[256,768]{1,0:T(8,128)(2,1)S(1)}, u32[]{:S(2)}, u32[]{:S(2)}) %collective-permute-start.2) | collective-permute-done | bytes 393248 | tf_op jit(solution)/shard_map/rows_second/ppermute | solution.py:382
  94.9 2.7 %collective-permute-start.5 = (bf16[256,768]{1,0:T(8,128)(2,1)S(1)}, bf16[256,768]{1,0:T(8,128)(2,1)S(1)}, u32[]{:S(2)}, u32[]{:S(2)}) collective-permute-start(bf16[256,768]{1,0:T(8,128)(2,1)S(1)} %collective-permute-done.4.refs_5_.refs_9_), channel_id=1, source_target_pairs={{0,6},{1,7},{2,0},{3,1},{4,2},{5,3},{6,4},{7,5},{8,14},{9,15},{10,... | collective-permute-start | bytes 1179656 | tf_op jit(solution)/shard_map/rows_second/ppermute | solution.py:382
  97.5 2.8 %collective-permute-start.14 = (bf16[256,768]{1,0:T(8,128)(2,1)S(1)}, bf16[256,768]{1,0:T(8,128)(2,1)S(1)}, u32[]{:S(2)}, u32[]{:S(2)}) collective-permute-start(bf16[256,768]{1,0:T(8,128)(2,1)S(1)} %collective-permute-done.1.refs_2_.refs_6_), channel_id=1, source_target_pairs={{0,1},{1,0},{2,3},{3,2},{4,5},{5,4},{6,7},{7,6},{8,9},{9,8},{10,11... | collective-permute-start | bytes 1179656 | tf_op jit(solution)/shard_map/rows_second/ppermute | solution.py:382
  100.5 2.6 %collective-permute-done.6.refs_7_.refs_11_ = bf16[256,768]{1,0:T(8,128)(2,1)S(1)} collective-permute-done((bf16[256,768]{1,0:T(8,128)(2,1)S(1)}, bf16[256,768]{1,0:T(8,128)(2,1)S(1)}, u32[]{:S(2)}, u32[]{:S(2)}) %collective-permute-start.6) | collective-permute-done | bytes 393248 | tf_op jit(solution)/shard_map/rows_second/ppermute | solution.py:382
  103.1 2.8 %collective-permute-start.17 = (bf16[256,768]{1,0:T(8,128)(2,1)S(1)}, bf16[256,768]{1,0:T(8,128)(2,1)S(1)}, u32[]{:S(2)}, u32[]{:S(2)}) collective-permute-start(bf16[256,768]{1,0:T(8,128)(2,1)S(1)} %collective-permute-done.4.refs_5_.refs_9_), channel_id=1, source_target_pairs={{0,1},{1,0},{2,3},{3,2},{4,5},{5,4},{6,7},{7,6},{8,9},{9,8},{10,11... | collective-permute-start | bytes 1179656 | tf_op jit(solution)/shard_map/rows_second/ppermute | solution.py:382
  106.0 1.6 collective-permute-start.15
  108.2 3.0 %collective-permute-start.9 = (bf16[80,768]{1,0:T(8,128)(2,1)S(1)}, bf16[80,768]{1,0:T(8,128)(2,1)}, u32[]{:S(2)}, u32[]{:S(2)}) collective-permute-start(bf16[80,768]{1,0:T(8,128)(2,1)S(1)} %slice.14), channel_id=1, source_target_pairs={{0,6},{1,7},{2,0},{3,1},{4,2},{5,3},{6,4},{7,5},{8,14},{9,15},{10,... | collective-permute-start | bytes 368648 | tf_op jit(solution)/shard_map/rows_second/ppermute | solution.py:382
  111.4 0.9 collective-permute-start.7
  112.3 1.6 collective-permute-done.9.refs_10_.refs_14_
  113.9 1.1 collective-permute-start.21
  115.3 3.5 %collective-permute-start.20 = (bf16[96,768]{1,0:T(8,128)(2,1)S(1)}, bf16[96,768]{1,0:T(8,128)(2,1)}, u32[]{:S(2)}, u32[]{:S(2)}) collective-permute-start(bf16[96,768]{1,0:T(8,128)(2,1)S(1)} %collective-permute-done.7.refs_8_.refs_12_), channel_id=1, source_target_pairs={{0,1},{1,0},{2,3},{3,2},{4,5},{5,4},{6,7},{7,6},{8,9},{9,8},{10,11... | collective-permute-start | bytes 442376 | tf_op jit(solution)/shard_map/rows_second/ppermute | solution.py:382
  118.9 0.6 copy-done.19
  119.6 3.5 %pick.1 = (bf16[512,768]{1,0:T(8,128)(2,1)}, bf16[256,768]{1,0:T(8,128)(2,1)}, bf16[256,768]{1,0:T(8,128)(2,1)}, bf16[256,768]{1,0:T(8,128)(2,1)}) custom-call(s32[5]{0:T(128)} %stack.23.refs_0_.spot_ref, bf16[256,768]{1,0:T(8,128)(2,1)} %copy-done, bf16[256,768]{1,0:T(8,128)(2,1)} %copy-done.7, bf16[256,768]{1,0:T(8,128)(2,1)} %copy-done.2, ...), custom_call_target="tpu_custom_call" | custom-call | bytes 3932160 | tf_op jit(solution)/shard_map/hessian_rows/pick/pallas_call | solution.py:240
  123.2 1.3 collective-permute-start.10
  124.4 2.5 %collective-permute-start.11 = (bf16[256,768]{1,0:T(8,128)(2,1)}, bf16[256,768]{1,0:T(8,128)(2,1)S(1)}, u32[]{:S(2)}, u32[]{:S(2)}) collective-permute-start(bf16[256,768]{1,0:T(8,128)(2,1)} %get-tuple-element.15), channel_id=1, source_target_pairs={{0,64},{32,96},{64,0},{96,32},{1,65},{33,97},{65,1},{97,33},{2,66}... | collective-permute-start | bytes 1179656 | tf_op jit(solution)/shard_map/hessian_rows/ppermute | solution.py:367
  127.0 1.1 collective-permute-start.12
  128.1 14.2 %layer.3 = (bf16[256,768]{1,0:T(8,128)(2,1)}, f32[8,256]{1,0:T(8,128)}) custom-call(s32[5]{0:T(128)} %stack.23.refs_0_.spot_ref, bf16[3,12288,256]{2,1,0:T(8,128)(2,1)} %build_dense.1.refs_1_, f32[16,1,768]{2,1,0:T(1,128)} %copy-done.10, bf16[256,768]{1,0:T(8,128)(2,1)} %copy-done, bf16[256,768]{1,0:T(8,128)(2,1)} %get-tuple-element.12.refs_4_, ...), custom_call_target="tpu_custom_call" | custom-call | flops 4831838208 | bytes 25165824 | tf_op jit(solution)/shard_map/layer_second/layer/pallas_call | solution.py:181
  142.2 2.1 %collective-permute-done.11.refs_1_ = bf16[256,768]{1,0:T(8,128)(2,1)S(1)} collective-permute-done((bf16[256,768]{1,0:T(8,128)(2,1)}, bf16[256,768]{1,0:T(8,128)(2,1)S(1)}, u32[]{:S(2)}, u32[]{:S(2)}) %collective-permute-start.11) | collective-permute-done | bytes 393248 | tf_op jit(solution)/shard_map/hessian_rows/ppermute | solution.py:367
  144.3 0.7 copy-done.13
  145.2 0.9 collective-permute-start.28
  146.1 1.1 collective-permute-start.29
  147.3 2.8 %collective-permute-start.30 = (f32[8,256]{1,0:T(8,128)}, f32[8,256]{1,0:T(8,128)S(1)}, u32[]{:S(2)}, u32[]{:S(2)}) collective-permute-start(f32[8,256]{1,0:T(8,128)} %get-tuple-element.17.refs_3_.refs_14_), channel_id=1, source_target_pairs={{0,64},{32,96},{64,0},{96,32},{1,65},{33,97},{65,1},{97,33},{2,66}... | collective-permute-start | bytes 24584 | tf_op jit(solution)/shard_map/layer_second/ppermute | solution.py:367
  150.2 2.7 %collective-permute-start.23 = (bf16[512,768]{1,0:T(8,128)(2,1)S(1)}, bf16[512,768]{1,0:T(8,128)(2,1)S(1)}, u32[]{:S(2)}, u32[]{:S(2)}) collective-permute-start(bf16[512,768]{1,0:T(8,128)(2,1)S(1)} %copy-done.24), channel_id=1, source_target_pairs={{0,1},{1,0},{2,3},{3,2},{4,5},{5,4},{6,7},{7,6},{8,9},{9,8},{10,11... | collective-permute-start | bytes 2359304 | tf_op jit(solution)/shard_map/hessian/ppermute | solution.py:382
  152.9 0.8 collective-permute-start.32
  153.7 1.7 collective-permute-start.24
  155.4 1.6 collective-permute-start.25
  157.0 6.8 %collective-permute-done.27.refs_8_ = bf16[256,768]{1,0:T(8,128)(2,1)S(1)} collective-permute-done((bf16[256,768]{1,0:T(8,128)(2,1)}, bf16[256,768]{1,0:T(8,128)(2,1)S(1)}, u32[]{:S(2)}, u32[]{:S(2)}) %collective-permute-start.27) | collective-permute-done | bytes 393248 | tf_op jit(solution)/shard_map/hessian/ppermute | solution.py:392
  163.8 0.9 collective-permute-start.26
  164.7 1.3 collective-permute-start.34
  166.5 1.0 collective-permute-done.34.refs_12_
  167.5 0.9 collective-permute-done.33.refs_11_
  168.4 0.7 copy-done.31
  169.2 13.6 %gram.1 = f32[3072,768]{1,0:T(8,128)} custom-call(s32[5]{0:T(128)} %stack.23.refs_0_.spot_ref, bf16[512,768]{1,0:T(8,128)(2,1)} %get-tuple-element.13.refs_0_, bf16[256,768]{1,0:T(8,128)(2,1)} %get-tuple-element.18.refs_1_, bf16[256,768]{1,0:T(8,128)(2,1)} %get-tuple-element.19.refs_2_, bf16[256,768]{1,0:T(8,128)(2,1)} %get-tuple-element.20.refs_3_, ...), custom_call_target="tpu_custom_call" | custom-call | flops 4831838208 | bytes 17301504 | tf_op jit(solution)/shard_map/hessian/gram/pallas_call | solution.py:341
  (112 shorter events, 3.9 us)
Async XLA Ops:
  7.2 23.3 %copy-start.23 = (s32[1,12,48]{2,0,1:T(1,128)S(1)}, s32[1,12,48]{2,0,1:T(1,128)}, u32[]{:S(2)}) copy-start(s32[1,12,48]{2,0,1:T(1,128)} %param.7) | copy-start | bytes 6916
  7.2 48.6 %all-gather.4.cloned.1.call-start = ((), (), s32[]{:S(2)}) async-start(), calls=%async_computation.1 | async-start | bytes 6684672 | tf_op jit(solution)/shard_map/rows_first/all_gather | solution.py:426
  9.3 36.2 %all-to-all-start = ((f32[16,1,768]{2,1,0:T(1,128)}), f32[16,1,768]{2,1,0:T(1,128)S(1)}, u32[]{:S(2)}, u32[]{:S(2)}) async-start(f32[16,1,768]{2,1,0:T(1,128)} %broadcast_in_dim.13), calls=%async_computation | async-start | bytes 98304 | tf_op jit(solution)/shard_map/gains/all_to_all | solution.py:428
  16.6 103.0 %all-gather.6.cloned.1.call-start = ((), (), s32[]{:S(2)}) async-start(), calls=%async_computation.2 | async-start | bytes 1966080 | tf_op jit(solution)/shard_map/columns/all_gather | solution.py:440
  45.5 37.2 %copy-start.1 = (bf16[4,64,768]{2,1,0:T(8,128)(2,1)S(1)}, bf16[4,64,768]{2,1,0:T(8,128)(2,1)}, u32[]{:S(2)}) copy-start(bf16[4,64,768]{2,1,0:T(8,128)(2,1)} %param.4) | copy-start | bytes 1179652
  69.7 13.1 %collective-permute-start = (bf16[256,768]{1,0:T(8,128)(2,1)}, bf16[256,768]{1,0:T(8,128)(2,1)S(1)}, u32[]{:S(2)}, u32[]{:S(2)}) collective-permute-start(bf16[256,768]{1,0:T(8,128)(2,1)} %get-tuple-element.12.refs_4_), channel_id=1, source_target_pairs={{0,16},{1,17},{2,18},{3,19},{4,20},{5,21},{6,22},{7,23},{8,24},{9,... | collective-permute-start | bytes 1179656 | tf_op jit(solution)/shard_map/hand_over/ppermute | solution.py:437
  83.5 36.0 %copy-start = (bf16[256,768]{1,0:T(8,128)(2,1)}, bf16[256,768]{1,0:T(8,128)(2,1)S(1)}, u32[]{:S(2)}) copy-start(bf16[256,768]{1,0:T(8,128)(2,1)S(1)} %get-tuple-element.23.refs_1_.refs_3_.refs_5_) | copy-start | bytes 1179652
  83.6 10.8 %collective-permute-start.2 = (bf16[256,768]{1,0:T(8,128)(2,1)S(1)}, bf16[256,768]{1,0:T(8,128)(2,1)S(1)}, u32[]{:S(2)}, u32[]{:S(2)}) collective-permute-start(bf16[256,768]{1,0:T(8,128)(2,1)S(1)} %get-tuple-element.23.refs_1_.refs_3_.refs_5_), channel_id=1, source_target_pairs={{0,2},{1,3},{2,4},{3,5},{4,6},{5,7},{6,0},{7,1},{8,10},{9,11},{10,... | collective-permute-start | bytes 1179656 | tf_op jit(solution)/shard_map/rows_second/ppermute | solution.py:382
  84.8 10.0 %collective-permute-start.4 = (bf16[256,768]{1,0:T(8,128)(2,1)S(1)}, bf16[256,768]{1,0:T(8,128)(2,1)S(1)}, u32[]{:S(2)}, u32[]{:S(2)}) collective-permute-start(bf16[256,768]{1,0:T(8,128)(2,1)S(1)} %get-tuple-element.23.refs_1_.refs_3_.refs_5_), channel_id=1, source_target_pairs={{0,8},{1,9},{2,10},{3,11},{4,12},{5,13},{6,14},{7,15},{8,0},{9,1},... | collective-permute-start | bytes 1179656 | tf_op jit(solution)/shard_map/rows_second/ppermute | solution.py:382
  85.3 12.2 %collective-permute-start.1 = (bf16[256,768]{1,0:T(8,128)(2,1)S(1)}, bf16[256,768]{1,0:T(8,128)(2,1)S(1)}, u32[]{:S(2)}, u32[]{:S(2)}) collective-permute-start(bf16[256,768]{1,0:T(8,128)(2,1)S(1)} %get-tuple-element.23.refs_1_.refs_3_.refs_5_), channel_id=1, source_target_pairs={{0,6},{1,7},{2,0},{3,1},{4,2},{5,3},{6,4},{7,5},{8,14},{9,15},{10,... | collective-permute-start | bytes 1179656 | tf_op jit(solution)/shard_map/rows_second/ppermute | solution.py:382
  86.8 13.6 %collective-permute-start.13 = (bf16[256,768]{1,0:T(8,128)(2,1)S(1)}, bf16[256,768]{1,0:T(8,128)(2,1)S(1)}, u32[]{:S(2)}, u32[]{:S(2)}) collective-permute-start(bf16[256,768]{1,0:T(8,128)(2,1)S(1)} %get-tuple-element.23.refs_1_.refs_3_.refs_5_), channel_id=1, source_target_pairs={{0,1},{1,0},{2,3},{3,2},{4,5},{5,4},{6,7},{7,6},{8,9},{9,8},{10,11... | collective-permute-start | bytes 1179656 | tf_op jit(solution)/shard_map/rows_second/ppermute | solution.py:382
  94.4 25.2 %copy-start.5 = (bf16[256,768]{1,0:T(8,128)(2,1)}, bf16[256,768]{1,0:T(8,128)(2,1)S(1)}, u32[]{:S(2)}) copy-start(bf16[256,768]{1,0:T(8,128)(2,1)S(1)} %collective-permute-done.2.refs_4_.refs_8_) | copy-start | bytes 1179652
  94.4 8.7 %collective-permute-start.6 = (bf16[256,768]{1,0:T(8,128)(2,1)S(1)}, bf16[256,768]{1,0:T(8,128)(2,1)S(1)}, u32[]{:S(2)}, u32[]{:S(2)}) collective-permute-start(bf16[256,768]{1,0:T(8,128)(2,1)S(1)} %collective-permute-done.2.refs_4_.refs_8_), channel_id=1, source_target_pairs={{0,8},{1,9},{2,10},{3,11},{4,12},{5,13},{6,14},{7,15},{8,0},{9,1},... | collective-permute-start | bytes 1179656 | tf_op jit(solution)/shard_map/rows_second/ppermute | solution.py:382
  94.8 11.1 %collective-permute-start.3 = (bf16[256,768]{1,0:T(8,128)(2,1)S(1)}, bf16[256,768]{1,0:T(8,128)(2,1)S(1)}, u32[]{:S(2)}, u32[]{:S(2)}) collective-permute-start(bf16[256,768]{1,0:T(8,128)(2,1)S(1)} %collective-permute-done.2.refs_4_.refs_8_), channel_id=1, source_target_pairs={{0,2},{1,3},{2,4},{3,5},{4,6},{5,7},{6,0},{7,1},{8,10},{9,11},{10,... | collective-permute-start | bytes 1179656 | tf_op jit(solution)/shard_map/rows_second/ppermute | solution.py:382
  94.9 24.7 %copy-start.6 = (bf16[256,768]{1,0:T(8,128)(2,1)}, bf16[256,768]{1,0:T(8,128)(2,1)S(1)}, u32[]{:S(2)}) copy-start(bf16[256,768]{1,0:T(8,128)(2,1)S(1)} %collective-permute-done.4.refs_5_.refs_9_) | copy-start | bytes 1179652
  94.9 11.2 %collective-permute-start.5 = (bf16[256,768]{1,0:T(8,128)(2,1)S(1)}, bf16[256,768]{1,0:T(8,128)(2,1)S(1)}, u32[]{:S(2)}, u32[]{:S(2)}) collective-permute-start(bf16[256,768]{1,0:T(8,128)(2,1)S(1)} %collective-permute-done.4.refs_5_.refs_9_), channel_id=1, source_target_pairs={{0,6},{1,7},{2,0},{3,1},{4,2},{5,3},{6,4},{7,5},{8,14},{9,15},{10,... | collective-permute-start | bytes 1179656 | tf_op jit(solution)/shard_map/rows_second/ppermute | solution.py:382
  97.5 22.0 %copy-start.7 = (bf16[256,768]{1,0:T(8,128)(2,1)}, bf16[256,768]{1,0:T(8,128)(2,1)S(1)}, u32[]{:S(2)}) copy-start(bf16[256,768]{1,0:T(8,128)(2,1)S(1)} %collective-permute-done.1.refs_2_.refs_6_) | copy-start | bytes 1179652
  97.5 10.2 %collective-permute-start.14 = (bf16[256,768]{1,0:T(8,128)(2,1)S(1)}, bf16[256,768]{1,0:T(8,128)(2,1)S(1)}, u32[]{:S(2)}, u32[]{:S(2)}) collective-permute-start(bf16[256,768]{1,0:T(8,128)(2,1)S(1)} %collective-permute-done.1.refs_2_.refs_6_), channel_id=1, source_target_pairs={{0,1},{1,0},{2,3},{3,2},{4,5},{5,4},{6,7},{7,6},{8,9},{9,8},{10,11... | collective-permute-start | bytes 1179656 | tf_op jit(solution)/shard_map/rows_second/ppermute | solution.py:382
  100.4 7.4 %collective-permute-start.16 = (bf16[256,768]{1,0:T(8,128)(2,1)S(1)}, bf16[256,768]{1,0:T(8,128)(2,1)S(1)}, u32[]{:S(2)}, u32[]{:S(2)}) collective-permute-start(bf16[256,768]{1,0:T(8,128)(2,1)S(1)} %collective-permute-done.2.refs_4_.refs_8_), channel_id=1, source_target_pairs={{0,1},{1,0},{2,3},{3,2},{4,5},{5,4},{6,7},{7,6},{8,9},{9,8},{10,11... | collective-permute-start | bytes 1179656 | tf_op jit(solution)/shard_map/rows_second/ppermute | solution.py:382
  103.1 16.5 %copy-start.3 = (bf16[256,768]{1,0:T(8,128)(2,1)}, bf16[256,768]{1,0:T(8,128)(2,1)S(1)}, u32[]{:S(2)}) copy-start(bf16[256,768]{1,0:T(8,128)(2,1)S(1)} %collective-permute-done.6.refs_7_.refs_11_) | copy-start | bytes 1179652
  103.1 5.1 %collective-permute-start.17 = (bf16[256,768]{1,0:T(8,128)(2,1)S(1)}, bf16[256,768]{1,0:T(8,128)(2,1)S(1)}, u32[]{:S(2)}, u32[]{:S(2)}) collective-permute-start(bf16[256,768]{1,0:T(8,128)(2,1)S(1)} %collective-permute-done.4.refs_5_.refs_9_), channel_id=1, source_target_pairs={{0,1},{1,0},{2,3},{3,2},{4,5},{5,4},{6,7},{7,6},{8,9},{9,8},{10,11... | collective-permute-start | bytes 1179656 | tf_op jit(solution)/shard_map/rows_second/ppermute | solution.py:382
  105.9 13.7 %copy-start.2 = (bf16[256,768]{1,0:T(8,128)(2,1)}, bf16[256,768]{1,0:T(8,128)(2,1)S(1)}, u32[]{:S(2)}) copy-start(bf16[256,768]{1,0:T(8,128)(2,1)S(1)} %collective-permute-done.3.refs_3_.refs_7_) | copy-start | bytes 1179652
  105.9 5.4 %collective-permute-start.8 = (bf16[80,768]{1,0:T(8,128)(2,1)S(1)}, bf16[80,768]{1,0:T(8,128)(2,1)S(1)}, u32[]{:S(2)}, u32[]{:S(2)}) collective-permute-start(bf16[80,768]{1,0:T(8,128)(2,1)S(1)} %slice.13), channel_id=1, source_target_pairs={{0,2},{1,3},{2,4},{3,5},{4,6},{5,7},{6,0},{7,1},{8,10},{9,11},{10,... | collective-permute-start | bytes 368648 | tf_op jit(solution)/shard_map/rows_second/ppermute | solution.py:382
  106.0 20.9 %collective-permute-start.15 = (bf16[256,768]{1,0:T(8,128)(2,1)S(1)}, bf16[256,768]{1,0:T(8,128)(2,1)}, u32[]{:S(2)}, u32[]{:S(2)}) collective-permute-start(bf16[256,768]{1,0:T(8,128)(2,1)S(1)} %collective-permute-done.3.refs_3_.refs_7_), channel_id=1, source_target_pairs={{0,1},{1,0},{2,3},{3,2},{4,5},{5,4},{6,7},{7,6},{8,9},{9,8},{10,11... | collective-permute-start | bytes 1179656 | tf_op jit(solution)/shard_map/rows_second/ppermute | solution.py:382
  107.7 20.4 %collective-permute-start.18 = (bf16[256,768]{1,0:T(8,128)(2,1)S(1)}, bf16[256,768]{1,0:T(8,128)(2,1)}, u32[]{:S(2)}, u32[]{:S(2)}) collective-permute-start(bf16[256,768]{1,0:T(8,128)(2,1)S(1)} %collective-permute-done.5.refs_6_.refs_10_), channel_id=1, source_target_pairs={{0,1},{1,0},{2,3},{3,2},{4,5},{5,4},{6,7},{7,6},{8,9},{9,8},{10,11... | collective-permute-start | bytes 1179656 | tf_op jit(solution)/shard_map/rows_second/ppermute | solution.py:382
  107.8 20.3 %collective-permute-start.19 = (bf16[256,768]{1,0:T(8,128)(2,1)S(1)}, bf16[256,768]{1,0:T(8,128)(2,1)}, u32[]{:S(2)}, u32[]{:S(2)}) collective-permute-start(bf16[256,768]{1,0:T(8,128)(2,1)S(1)} %collective-permute-done.6.refs_7_.refs_11_), channel_id=1, source_target_pairs={{0,1},{1,0},{2,3},{3,2},{4,5},{5,4},{6,7},{7,6},{8,9},{9,8},{10,11... | collective-permute-start | bytes 1179656 | tf_op jit(solution)/shard_map/rows_second/ppermute | solution.py:382
  108.2 5.6 %collective-permute-start.9 = (bf16[80,768]{1,0:T(8,128)(2,1)S(1)}, bf16[80,768]{1,0:T(8,128)(2,1)}, u32[]{:S(2)}, u32[]{:S(2)}) collective-permute-start(bf16[80,768]{1,0:T(8,128)(2,1)S(1)} %slice.14), channel_id=1, source_target_pairs={{0,6},{1,7},{2,0},{3,1},{4,2},{5,3},{6,4},{7,5},{8,14},{9,15},{10,... | collective-permute-start | bytes 368648 | tf_op jit(solution)/shard_map/rows_second/ppermute | solution.py:382
  111.4 4.0 %collective-permute-start.7 = (bf16[96,768]{1,0:T(8,128)(2,1)S(1)}, bf16[96,768]{1,0:T(8,128)(2,1)S(1)}, u32[]{:S(2)}, u32[]{:S(2)}) collective-permute-start(bf16[96,768]{1,0:T(8,128)(2,1)S(1)} %slice.12), channel_id=1, source_target_pairs={{0,8},{1,9},{2,10},{3,11},{4,12},{5,13},{6,14},{7,15},{8,0},{9,1},... | collective-permute-start | bytes 442376 | tf_op jit(solution)/shard_map/rows_second/ppermute | solution.py:382
  113.9 5.0 %collective-permute-start.21 = (bf16[80,768]{1,0:T(8,128)(2,1)S(1)}, bf16[80,768]{1,0:T(8,128)(2,1)S(1)}, u32[]{:S(2)}, u32[]{:S(2)}) collective-permute-start(bf16[80,768]{1,0:T(8,128)(2,1)S(1)} %collective-permute-done.8.refs_9_.refs_13_), channel_id=1, source_target_pairs={{0,1},{1,0},{2,3},{3,2},{4,5},{5,4},{6,7},{7,6},{8,9},{9,8},{10,11... | collective-permute-start | bytes 368648 | tf_op jit(solution)/shard_map/rows_second/ppermute | solution.py:382
  115.3 9.1 %collective-permute-start.20 = (bf16[96,768]{1,0:T(8,128)(2,1)S(1)}, bf16[96,768]{1,0:T(8,128)(2,1)}, u32[]{:S(2)}, u32[]{:S(2)}) collective-permute-start(bf16[96,768]{1,0:T(8,128)(2,1)S(1)} %collective-permute-done.7.refs_8_.refs_12_), channel_id=1, source_target_pairs={{0,1},{1,0},{2,3},{3,2},{4,5},{5,4},{6,7},{7,6},{8,9},{9,8},{10,11... | collective-permute-start | bytes 442376 | tf_op jit(solution)/shard_map/rows_second/ppermute | solution.py:382
  119.5 3.7 %collective-permute-start.22 = (bf16[80,768]{1,0:T(8,128)(2,1)}, bf16[80,768]{1,0:T(8,128)(2,1)}, u32[]{:S(2)}, u32[]{:S(2)}) collective-permute-start(bf16[80,768]{1,0:T(8,128)(2,1)} %collective-permute-done.9.refs_10_.refs_14_), channel_id=1, source_target_pairs={{0,1},{1,0},{2,3},{3,2},{4,5},{5,4},{6,7},{7,6},{8,9},{9,8},{10,11... | collective-permute-start | bytes 368648 | tf_op jit(solution)/shard_map/rows_second/ppermute | solution.py:382
  123.2 19.1 %collective-permute-start.10 = (bf16[256,768]{1,0:T(8,128)(2,1)}, bf16[256,768]{1,0:T(8,128)(2,1)S(1)}, u32[]{:S(2)}, u32[]{:S(2)}) collective-permute-start(bf16[256,768]{1,0:T(8,128)(2,1)} %get-tuple-element.14), channel_id=1, source_target_pairs={{0,32},{32,64},{64,96},{96,0},{1,33},{33,65},{65,97},{97,1},{2,34}... | collective-permute-start | bytes 1179656 | tf_op jit(solution)/shard_map/hessian_rows/ppermute | solution.py:367
  124.4 19.9 %collective-permute-start.11 = (bf16[256,768]{1,0:T(8,128)(2,1)}, bf16[256,768]{1,0:T(8,128)(2,1)S(1)}, u32[]{:S(2)}, u32[]{:S(2)}) collective-permute-start(bf16[256,768]{1,0:T(8,128)(2,1)} %get-tuple-element.15), channel_id=1, source_target_pairs={{0,64},{32,96},{64,0},{96,32},{1,65},{33,97},{65,1},{97,33},{2,66}... | collective-permute-start | bytes 1179656 | tf_op jit(solution)/shard_map/hessian_rows/ppermute | solution.py:367
  127.0 23.2 %copy-start.24 = (bf16[512,768]{1,0:T(8,128)(2,1)S(1)}, bf16[512,768]{1,0:T(8,128)(2,1)}, u32[]{:S(2)}) copy-start(bf16[512,768]{1,0:T(8,128)(2,1)} %get-tuple-element.13.refs_0_) | copy-start | bytes 2359300
  127.0 17.4 %collective-permute-start.12 = (bf16[256,768]{1,0:T(8,128)(2,1)}, bf16[256,768]{1,0:T(8,128)(2,1)S(1)}, u32[]{:S(2)}, u32[]{:S(2)}) collective-permute-start(bf16[256,768]{1,0:T(8,128)(2,1)} %get-tuple-element.16), channel_id=1, source_target_pairs={{0,96},{32,0},{64,32},{96,64},{1,97},{33,1},{65,33},{97,65},{2,98}... | collective-permute-start | bytes 1179656 | tf_op jit(solution)/shard_map/hessian_rows/ppermute | solution.py:367
  145.2 10.2 %collective-permute-start.28 = (bf16[256,768]{1,0:T(8,128)(2,1)}, bf16[256,768]{1,0:T(8,128)(2,1)S(1)}, u32[]{:S(2)}, u32[]{:S(2)}) collective-permute-start(bf16[256,768]{1,0:T(8,128)(2,1)} %get-tuple-element.19.refs_2_), channel_id=1, source_target_pairs={{0,8},{1,9},{2,10},{3,11},{4,12},{5,13},{6,14},{7,15},{8,0},{9,1},... | collective-permute-start | bytes 1179656 | tf_op jit(solution)/shard_map/hessian/ppermute | solution.py:392
  146.1 6.8 %collective-permute-start.29 = (f32[8,256]{1,0:T(8,128)}, f32[8,256]{1,0:T(8,128)S(1)}, u32[]{:S(2)}, u32[]{:S(2)}) collective-permute-start(f32[8,256]{1,0:T(8,128)} %get-tuple-element.17.refs_3_.refs_14_), channel_id=1, source_target_pairs={{0,32},{32,64},{64,96},{96,0},{1,33},{33,65},{65,97},{97,1},{2,34}... | collective-permute-start | bytes 24584 | tf_op jit(solution)/shard_map/layer_second/ppermute | solution.py:367
  147.3 5.6 %collective-permute-start.30 = (f32[8,256]{1,0:T(8,128)}, f32[8,256]{1,0:T(8,128)S(1)}, u32[]{:S(2)}, u32[]{:S(2)}) collective-permute-start(f32[8,256]{1,0:T(8,128)} %get-tuple-element.17.refs_3_.refs_14_), channel_id=1, source_target_pairs={{0,64},{32,96},{64,0},{96,32},{1,65},{33,97},{65,1},{97,33},{2,66}... | collective-permute-start | bytes 24584 | tf_op jit(solution)/shard_map/layer_second/ppermute | solution.py:367
  150.0 3.7 %collective-permute-start.31 = (f32[8,256]{1,0:T(8,128)}, f32[8,256]{1,0:T(8,128)S(1)}, u32[]{:S(2)}, u32[]{:S(2)}) collective-permute-start(f32[8,256]{1,0:T(8,128)} %get-tuple-element.17.refs_3_.refs_14_), channel_id=1, source_target_pairs={{0,96},{32,0},{64,32},{96,64},{1,97},{33,1},{65,33},{97,65},{2,98}... | collective-permute-start | bytes 24584 | tf_op jit(solution)/shard_map/layer_second/ppermute | solution.py:367
  150.2 16.3 %collective-permute-start.23 = (bf16[512,768]{1,0:T(8,128)(2,1)S(1)}, bf16[512,768]{1,0:T(8,128)(2,1)S(1)}, u32[]{:S(2)}, u32[]{:S(2)}) collective-permute-start(bf16[512,768]{1,0:T(8,128)(2,1)S(1)} %copy-done.24), channel_id=1, source_target_pairs={{0,1},{1,0},{2,3},{3,2},{4,5},{5,4},{6,7},{7,6},{8,9},{9,8},{10,11... | collective-permute-start | bytes 2359304 | tf_op jit(solution)/shard_map/hessian/ppermute | solution.py:382
  152.9 10.9 %collective-permute-start.27 = (bf16[256,768]{1,0:T(8,128)(2,1)}, bf16[256,768]{1,0:T(8,128)(2,1)S(1)}, u32[]{:S(2)}, u32[]{:S(2)}) collective-permute-start(bf16[256,768]{1,0:T(8,128)(2,1)} %get-tuple-element.18.refs_1_), channel_id=1, source_target_pairs={{0,2},{1,3},{2,0},{3,1},{4,6},{5,7},{6,4},{7,5},{8,10},{9,11},{10,... | collective-permute-start | bytes 1179656 | tf_op jit(solution)/shard_map/hessian/ppermute | solution.py:392
  152.9 11.7 %collective-permute-start.32 = (bf16[256,768]{1,0:T(8,128)(2,1)}, bf16[256,768]{1,0:T(8,128)(2,1)S(1)}, u32[]{:S(2)}, u32[]{:S(2)}) collective-permute-start(bf16[256,768]{1,0:T(8,128)(2,1)} %get-tuple-element.20.refs_3_), channel_id=1, source_target_pairs={{0,6},{1,7},{2,4},{3,5},{4,2},{5,3},{6,0},{7,1},{8,14},{9,15},{10,... | collective-permute-start | bytes 1179656 | tf_op jit(solution)/shard_map/hessian/ppermute | solution.py:392
  153.7 12.2 %collective-permute-start.24 = (bf16[256,768]{1,0:T(8,128)(2,1)}, bf16[256,768]{1,0:T(8,128)(2,1)S(1)}, u32[]{:S(2)}, u32[]{:S(2)}) collective-permute-start(bf16[256,768]{1,0:T(8,128)(2,1)} %get-tuple-element.18.refs_1_), channel_id=1, source_target_pairs={{0,1},{1,0},{2,3},{3,2},{4,5},{5,4},{6,7},{7,6},{8,9},{9,8},{10,11... | collective-permute-start | bytes 1179656 | tf_op jit(solution)/shard_map/hessian/ppermute | solution.py:382
  155.4 10.7 %collective-permute-start.25 = (bf16[256,768]{1,0:T(8,128)(2,1)}, bf16[256,768]{1,0:T(8,128)(2,1)}, u32[]{:S(2)}, u32[]{:S(2)}) collective-permute-start(bf16[256,768]{1,0:T(8,128)(2,1)} %get-tuple-element.19.refs_2_), channel_id=1, source_target_pairs={{0,1},{1,0},{2,3},{3,2},{4,5},{5,4},{6,7},{7,6},{8,9},{9,8},{10,11... | collective-permute-start | bytes 1179656 | tf_op jit(solution)/shard_map/hessian/ppermute | solution.py:382
  163.8 2.7 %collective-permute-start.26 = (bf16[256,768]{1,0:T(8,128)(2,1)}, bf16[256,768]{1,0:T(8,128)(2,1)S(1)}, u32[]{:S(2)}, u32[]{:S(2)}) collective-permute-start(bf16[256,768]{1,0:T(8,128)(2,1)} %get-tuple-element.20.refs_3_), channel_id=1, source_target_pairs={{0,1},{1,0},{2,3},{3,2},{4,5},{5,4},{6,7},{7,6},{8,9},{9,8},{10,11... | collective-permute-start | bytes 1179656 | tf_op jit(solution)/shard_map/hessian/ppermute | solution.py:382
  164.7 2.9 %collective-permute-start.34 = (bf16[256,768]{1,0:T(8,128)(2,1)}, bf16[256,768]{1,0:T(8,128)(2,1)S(1)}, u32[]{:S(2)}, u32[]{:S(2)}) collective-permute-start(bf16[256,768]{1,0:T(8,128)(2,1)} %after.3.refs_9_), channel_id=1, source_target_pairs={{0,1},{1,0},{2,3},{3,2},{4,5},{5,4},{6,7},{7,6},{8,9},{9,8},{10,11... | collective-permute-start | bytes 1179656 | tf_op jit(solution)/shard_map/hessian/ppermute | solution.py:382
  166.0 2.5 %collective-permute-start.33 = (bf16[256,768]{1,0:T(8,128)(2,1)S(1)}, bf16[256,768]{1,0:T(8,128)(2,1)S(1)}, u32[]{:S(2)}, u32[]{:S(2)}) collective-permute-start(bf16[256,768]{1,0:T(8,128)(2,1)S(1)} %collective-permute-done.27.refs_8_), channel_id=1, source_target_pairs={{0,1},{1,0},{2,3},{3,2},{4,5},{5,4},{6,7},{7,6},{8,9},{9,8},{10,11... | collective-permute-start | bytes 1179656 | tf_op jit(solution)/shard_map/hessian/ppermute | solution.py:382
  166.1 3.1 %collective-permute-start.35 = (bf16[256,768]{1,0:T(8,128)(2,1)S(1)}, bf16[256,768]{1,0:T(8,128)(2,1)}, u32[]{:S(2)}, u32[]{:S(2)}) collective-permute-start(bf16[256,768]{1,0:T(8,128)(2,1)S(1)} %collective-permute-done.32.refs_10_), channel_id=1, source_target_pairs={{0,1},{1,0},{2,3},{3,2},{4,5},{5,4},{6,7},{7,6},{8,9},{9,8},{10,11... | collective-permute-start | bytes 1179656 | tf_op jit(solution)/shard_map/hessian/ppermute | solution.py:382
  (23 other events, 108.8 us)
Sparse Core Ops, SparseCore 0:
  9.7 46.0 all-gather.3
  83.7 28.5 all-gather.5
